TPU v7x, 512 devices: a whole 4x8x8 slice. The times are simulated.
512 devices in a mesh: sea: 32 (over y, x_lo, core), fault: 16 (over z, x_hi).
Axes of the slice: x: 4 (x_hi: 2, x_lo: 2; x = x_hi * 2 + x_lo), y: 8, z: 8, core: 2. Of those that a mesh axis runs over, the one named last changes fastest.
Arguments:
- slip_rate: bfloat16 [65536, 128], P(('fault', 'sea')), may hold values from -6 to 6
- near_blocks: bfloat16 [32, 16, 8, 256, 256], P('sea', 'fault'), may hold values from -0.375 to 0.375
- near_rows: int32 [32, 16, 8], P('sea', 'fault'), may hold values from 0 to 15
- near_cols: int32 [32, 16, 8], P('sea', 'fault'), may hold values from 0 to 15
- near_scale: float32 [32, 16, 8], P('sea', 'fault'), may hold values from 0.1 to 0.5
- far_left: bfloat16 [32, 16, 24, 48, 256], P('sea', 'fault'), may hold values from -0.875 to 0.875
- far_right: bfloat16 [32, 16, 24, 48, 256], P('sea', 'fault'), may hold values from -0.375 to 0.375
- far_rows: int32 [32, 16, 24], P('sea', 'fault'), may hold values from 0 to 15
- far_cols: int32 [32, 16, 24], P('sea', 'fault'), may hold values from 0 to 15
- far_rank: int32 [32, 16, 24], P('sea', 'fault'), may hold values from 16 to 48, as said below
- far_scale: float32 [32, 16, 24], P('sea', 'fault'), may hold values from 0.1 to 0.5
- sea_depth: float32 [512, 256], P('sea', 'fault'), may hold values from 0.3 to 1
- wet_mask: int32 [512, 256], P('sea', 'fault'), may hold values 0 or 1
Outputs:
- uplift: float32 [512, 256, 128], P('sea', 'fault')
- sea_level: float32 [512, 256, 128], P('sea', 'fault')
Inputs may be any that keep to these rules, and one draw needn't show every extreme that they name: `far_rank`: block 0 of every device has rank 48; every rank is at least 16.
All inputs are finite; a program needn't handle non-finite values. No bound on the sum of `wet_mask` on one device may be relied on, other than what follows from the above.
Results may differ from a plain program's by a relative error of at most 0.0024.
Values may be sent and summed in bfloat16 or wider, within the bound.
A program may use at most 64 MiB of HBM per device.

v0:
```python
import jax
import jax.numpy as jnp
from jax import lax
from jax.sharding import PartitionSpec as P

STEPS = 6


gravity_step = 0.7
height_step = 0.7


def extended(cells, sides, width):
    for axis, dim in sides:
        count = lax.axis_size(axis)
        ends = count - 1
        head = lax.slice_in_dim(cells, 0, width, axis=dim)
        tail = lax.slice_in_dim(cells, cells.shape[dim] - width, cells.shape[dim], axis=dim)
        cells = jnp.concatenate(
            [
                lax.ppermute(tail, axis, [(i, (i + 1) % count) for i in range(ends)]),
                cells,
                lax.ppermute(head, axis, [((i + 1) % count, i) for i in range(ends)]),
            ],
            axis=dim,
        )
    return cells


def advance(height, east_flow, north_flow, depth_pad):
    new_east = east_flow[1:-1, :-1] - gravity_step * (height[1:-1, 1:] - height[1:-1, :-1])
    east_depth = jnp.minimum(depth_pad[1:-1, :-1], depth_pad[1:-1, 1:])
    flux_east = east_depth[:, :, None] * new_east
    new_north = north_flow[:-1, 1:-1] - gravity_step * (height[1:, 1:-1] - height[:-1, 1:-1])
    north_depth = jnp.minimum(depth_pad[:-1, 1:-1], depth_pad[1:, 1:-1])
    flux_north = north_depth[:, :, None] * new_north
    change = flux_east[:, 1:] - flux_east[:, :-1] + flux_north[1:] - flux_north[:-1]
    new_height = height[1:-1, 1:-1] - height_step * change
    return (new_height, new_east[:, 1:], new_north[1:])


def on_device(
    slip_rate,
    near_blocks,
    near_rows,
    near_cols,
    near_scale,
    far_left,
    far_right,
    far_rows,
    far_cols,
    far_rank,
    far_scale,
    sea_depth,
    wet_mask,
):
    brick_y, brick_x = sea_depth.shape
    fault_count = lax.axis_size("fault")
    leaf_size = near_blocks.shape[-1]
    rank_pad = far_left.shape[-2]
    members = slip_rate.shape[1]
    leaf_count = brick_y * brick_x * fault_count // leaf_size
    targets = jnp.arange(leaf_count)
    gathered = lax.all_gather(slip_rate, "sea", axis=0, tiled=True)
    leaves = gathered.reshape(-1, leaf_size, members)
    near_slip = leaves[near_cols[0, 0]]
    near_term = jnp.einsum(
        "bij,bjs->bis", near_blocks[0, 0], near_slip, preferred_element_type=jnp.float32
    )
    near_weight = (near_rows[0, 0][:, None] == targets).astype(jnp.float32) * near_scale[0, 0][
        :, None
    ]
    total = jnp.einsum("br,bis->ris", near_weight, near_term, precision=lax.Precision.HIGHEST)
    far_slip = leaves[far_cols[0, 0]]
    coeffs = jnp.einsum(
        "bkc,bcs->bks", far_right[0, 0], far_slip, preferred_element_type=jnp.float32
    )
    kept = jnp.arange(rank_pad)[None, :, None] < far_rank[0, 0][:, None, None]
    coeffs = jnp.where(kept, coeffs, jnp.float32(0.0)).astype(jnp.bfloat16)
    far_term = jnp.einsum(
        "bki,bks->bis", far_left[0, 0], coeffs, preferred_element_type=jnp.float32
    )
    far_weight = (far_rows[0, 0][:, None] == targets).astype(jnp.float32) * far_scale[0, 0][:, None]
    total = total + jnp.einsum("br,bis->ris", far_weight, far_term, precision=lax.Precision.HIGHEST)
    partial_value = total.reshape(brick_y, fault_count, brick_x, members)
    ordered = jnp.transpose(partial_value, (1, 0, 2, 3))
    summed = lax.psum_scatter(ordered, "fault", scatter_dimension=0, tiled=True)
    uplift = summed[0]
    wet = wet_mask.astype(jnp.float32)
    depth_cell = sea_depth * wet
    height = uplift * wet[:, :, None]
    east_flow = jnp.zeros_like(height)
    north_flow = jnp.zeros_like(height)
    depth_pad = extended(depth_cell, (("sea", 0), ("fault", 1)), 1)
    for step_index in range(STEPS):
        padded = (
            extended(height, (("sea", 0), ("fault", 1)), 1),
            extended(east_flow, (("sea", 0), ("fault", 1)), 1),
            extended(north_flow, (("sea", 0), ("fault", 1)), 1),
        )
        height, east_flow, north_flow = advance(padded[0], padded[1], padded[2], depth_pad)
    return (uplift, height)


def solution(mesh):
    placed = (
        P(("fault", "sea"), None),
        P("sea", "fault", None, None, None),
        P("sea", "fault", None),
        P("sea", "fault", None),
        P("sea", "fault", None),
        P("sea", "fault", None, None, None),
        P("sea", "fault", None, None, None),
        P("sea", "fault", None),
        P("sea", "fault", None),
        P("sea", "fault", None),
        P("sea", "fault", None),
        P("sea", "fault"),
        P("sea", "fault"),
    )
    return jax.shard_map(
        on_device,
        mesh=mesh,
        in_specs=placed,
        out_specs=(P("sea", "fault", None), P("sea", "fault", None)),
        check_vma=False,
    )
```

profile of v0, /device:TPU:288, one launch (start us, length us, event | category | flops | bytes accessed | tf_op | source)
XLA Modules:
  0.0 510.8 jit_solution(5362446358330737596)
XLA Ops:
  10.0 66.4 %all-gather.2.cloned.1.call-done = bf16[4096,128]{1,0:T(8,128)(2,1)} async-done(((bf16[128,128]{1,0:T(8,128)(2,1)}), bf16[4096,128]{1,0:T(8,128)(2,1)}) %all-gather.2.cloned.1.call-update) | async-done | bytes 1048592 | tf_op jit(solution)/shard_map/all_gather | solution.py:64
  76.4 2.1 gather_fusion.1
  78.5 3.8 fusion.5
  82.3 3.6 copy.17
  91.3 2.0 fusion.2
  93.3 2.0 copy.19
  95.3 2.1 collective-permute-start.4
  97.4 5.5 %collective-permute-start.5 = (f32[1,16,128]{2,1,0:T(8,128)S(1)}, f32[1,16,128]{2,1,0:T(8,128)S(1)}, u32[]{:S(2)}, u32[]{:S(2)}) collective-permute-start(f32[1,16,128]{2,1,0:T(8,128)S(1)} %broadcast.92), channel_id=1, source_target_pairs={{16,0},{32,16},{48,32},{64,48},{80,64},{96,80},{112,96},{128,112},... | collective-permute-start | bytes 24584 | tf_op jit(solution)/shard_map/ppermute | solution.py:23
  103.0 1.9 collective-permute-start
  105.0 5.8 %collective-permute-start.1 = (f32[1,16]{1,0:T(1,128)S(1)}, f32[1,16]{1,0:T(1,128)S(1)}, u32[]{:S(2)}, u32[]{:S(2)}) collective-permute-start(f32[1,16]{1,0:T(1,128)S(1)} %get-tuple-element.58), channel_id=1, source_target_pairs={{16,0},{32,16},{48,32},{64,48},{80,64},{96,80},{112,96},{128,112},... | collective-permute-start | bytes 200 | tf_op jit(solution)/shard_map/ppermute | solution.py:23
  112.1 4.9 collective-permute-start.2
  117.0 4.6 collective-permute-start.3
  121.6 2.5 collective-permute-done.3
  124.1 184.5 %reduce-scatter.2.cloned.1.call-done = f32[1,16,16,128]{3,2,1,0:T(8,128)} async-done(((f32[16,16,16,128]{3,2,1,0:T(8,128)}), f32[1,16,16,128]{3,2,1,0:T(8,128)}) %reduce-scatter.2.cloned.1.call-update) | async-done | bytes 131088 | tf_op jit(solution)/shard_map/reduce_scatter | solution.py:87
  309.7 1.9 collective-permute-start.7
  311.6 5.8 %collective-permute-start.8 = (f32[1,16,128]{2,1,0:T(8,128)S(1)}, f32[1,16,128]{2,1,0:T(8,128)S(1)}, u32[]{:S(2)}, u32[]{:S(2)}) collective-permute-start(f32[1,16,128]{2,1,0:T(8,128)S(1)} %get-tuple-element.54), channel_id=1, source_target_pairs={{16,0},{32,16},{48,32},{64,48},{80,64},{96,80},{112,96},{128,112},... | collective-permute-start | bytes 24584 | tf_op jit(solution)/shard_map/ppermute | solution.py:23
  317.4 2.5 collective-permute-start.6
  319.9 3.9 collective-permute-start.10
  323.8 5.6 %collective-permute-start.9 = (f32[18,1,128]{2,1,0:T(1,128)S(1)}, f32[18,1,128]{2,1,0:T(1,128)S(1)}, u32[]{:S(2)}, u32[]{:S(2)}) collective-permute-start(f32[18,1,128]{2,1,0:T(1,128)S(1)} %get-tuple-element.42), channel_id=1, source_target_pairs={{1,0},{2,1},{3,2},{4,3},{5,4},{6,5},{7,6},{8,7},{9,8},{10,9},{11,1... | collective-permute-start | bytes 27656 | tf_op jit(solution)/shard_map/ppermute | solution.py:23
  329.5 1.9 collective-permute-start.18
  331.6 1.9 collective-permute-start.11
  333.6 5.8 %collective-permute-start.12 = (f32[1,16,128]{2,1,0:T(8,128)S(1)}, f32[1,16,128]{2,1,0:T(8,128)S(1)}, u32[]{:S(2)}, u32[]{:S(2)}) collective-permute-start(f32[1,16,128]{2,1,0:T(8,128)S(1)} %get-tuple-element.31), channel_id=1, source_target_pairs={{16,0},{32,16},{48,32},{64,48},{80,64},{96,80},{112,96},{128,112},... | collective-permute-start | bytes 24584 | tf_op jit(solution)/shard_map/ppermute | solution.py:23
  339.5 1.9 collective-permute-start.14
  341.4 5.8 %collective-permute-start.15 = (f32[1,16,128]{2,1,0:T(8,128)S(1)}, f32[1,16,128]{2,1,0:T(8,128)S(1)}, u32[]{:S(2)}, u32[]{:S(2)}) collective-permute-start(f32[1,16,128]{2,1,0:T(8,128)S(1)} %get-tuple-element.52), channel_id=1, source_target_pairs={{16,0},{32,16},{48,32},{64,48},{80,64},{96,80},{112,96},{128,112},... | collective-permute-start | bytes 24584 | tf_op jit(solution)/shard_map/ppermute | solution.py:23
  347.2 4.5 collective-permute-start.13
  351.8 4.9 collective-permute-start.16
  356.7 2.4 collective-permute-start.17
  361.3 4.6 collective-permute-done.17
  366.0 1.9 collective-permute-start.19
  368.0 5.8 %collective-permute-start.20 = (f32[1,16,128]{2,1,0:T(8,128)S(1)}, f32[1,16,128]{2,1,0:T(8,128)S(1)}, u32[]{:S(2)}, u32[]{:S(2)}) collective-permute-start(f32[1,16,128]{2,1,0:T(8,128)S(1)} %get-tuple-element.29), channel_id=1, source_target_pairs={{16,0},{32,16},{48,32},{64,48},{80,64},{96,80},{112,96},{128,112},... | collective-permute-start | bytes 24584 | tf_op jit(solution)/shard_map/ppermute | solution.py:23
  375.7 5.8 %collective-permute-start.23 = (f32[1,16,128]{2,1,0:T(8,128)S(1)}, f32[1,16,128]{2,1,0:T(8,128)S(1)}, u32[]{:S(2)}, u32[]{:S(2)}) collective-permute-start(f32[1,16,128]{2,1,0:T(8,128)S(1)} %get-tuple-element.50), channel_id=1, source_target_pairs={{16,0},{32,16},{48,32},{64,48},{80,64},{96,80},{112,96},{128,112},... | collective-permute-start | bytes 24584 | tf_op jit(solution)/shard_map/ppermute | solution.py:23
  383.5 7.5 %collective-permute-start.24 = (f32[18,1,128]{2,1,0:T(1,128)S(1)}, f32[18,1,128]{2,1,0:T(1,128)S(1)}, u32[]{:S(2)}, u32[]{:S(2)}) collective-permute-start(f32[18,1,128]{2,1,0:T(1,128)S(1)} %get-tuple-element.38), channel_id=1, source_target_pairs={{1,0},{2,1},{3,2},{4,3},{5,4},{6,5},{7,6},{8,7},{9,8},{10,9},{11,1... | collective-permute-start | bytes 27656 | tf_op jit(solution)/shard_map/ppermute | solution.py:23
  395.1 5.1 %collective-permute-done.25 = f32[18,1,128]{2,1,0:T(1,128)S(1)} collective-permute-done((f32[18,1,128]{2,1,0:T(1,128)S(1)}, f32[18,1,128]{2,1,0:T(1,128)S(1)}, u32[]{:S(2)}, u32[]{:S(2)}) %collective-permute-start.25) | collective-permute-done | bytes 9248 | tf_op jit(solution)/shard_map/ppermute | solution.py:21
  400.4 1.9 collective-permute-start.27
  402.3 5.8 %collective-permute-start.28 = (f32[1,16,128]{2,1,0:T(8,128)S(1)}, f32[1,16,128]{2,1,0:T(8,128)S(1)}, u32[]{:S(2)}, u32[]{:S(2)}) collective-permute-start(f32[1,16,128]{2,1,0:T(8,128)S(1)} %get-tuple-element.27), channel_id=1, source_target_pairs={{16,0},{32,16},{48,32},{64,48},{80,64},{96,80},{112,96},{128,112},... | collective-permute-start | bytes 24584 | tf_op jit(solution)/shard_map/ppermute | solution.py:23
  410.1 5.8 %collective-permute-start.31 = (f32[1,16,128]{2,1,0:T(8,128)S(1)}, f32[1,16,128]{2,1,0:T(8,128)S(1)}, u32[]{:S(2)}, u32[]{:S(2)}) collective-permute-start(f32[1,16,128]{2,1,0:T(8,128)S(1)} %get-tuple-element.48), channel_id=1, source_target_pairs={{16,0},{32,16},{48,32},{64,48},{80,64},{96,80},{112,96},{128,112},... | collective-permute-start | bytes 24584 | tf_op jit(solution)/shard_map/ppermute | solution.py:23
  417.8 7.5 %collective-permute-start.32 = (f32[18,1,128]{2,1,0:T(1,128)S(1)}, f32[18,1,128]{2,1,0:T(1,128)S(1)}, u32[]{:S(2)}, u32[]{:S(2)}) collective-permute-start(f32[18,1,128]{2,1,0:T(1,128)S(1)} %get-tuple-element.36), channel_id=1, source_target_pairs={{1,0},{2,1},{3,2},{4,3},{5,4},{6,5},{7,6},{8,7},{9,8},{10,9},{11,1... | collective-permute-start | bytes 27656 | tf_op jit(solution)/shard_map/ppermute | solution.py:23
  429.4 5.1 %collective-permute-done.33 = f32[18,1,128]{2,1,0:T(1,128)S(1)} collective-permute-done((f32[18,1,128]{2,1,0:T(1,128)S(1)}, f32[18,1,128]{2,1,0:T(1,128)S(1)}, u32[]{:S(2)}, u32[]{:S(2)}) %collective-permute-start.33) | collective-permute-done | bytes 9248 | tf_op jit(solution)/shard_map/ppermute | solution.py:21
  434.7 1.9 collective-permute-start.35
  436.6 5.8 %collective-permute-start.36 = (f32[1,16,128]{2,1,0:T(8,128)S(1)}, f32[1,16,128]{2,1,0:T(8,128)S(1)}, u32[]{:S(2)}, u32[]{:S(2)}) collective-permute-start(f32[1,16,128]{2,1,0:T(8,128)S(1)} %get-tuple-element.25), channel_id=1, source_target_pairs={{16,0},{32,16},{48,32},{64,48},{80,64},{96,80},{112,96},{128,112},... | collective-permute-start | bytes 24584 | tf_op jit(solution)/shard_map/ppermute | solution.py:23
  444.4 5.8 %collective-permute-start.39 = (f32[1,16,128]{2,1,0:T(8,128)S(1)}, f32[1,16,128]{2,1,0:T(8,128)S(1)}, u32[]{:S(2)}, u32[]{:S(2)}) collective-permute-start(f32[1,16,128]{2,1,0:T(8,128)S(1)} %get-tuple-element.46), channel_id=1, source_target_pairs={{16,0},{32,16},{48,32},{64,48},{80,64},{96,80},{112,96},{128,112},... | collective-permute-start | bytes 24584 | tf_op jit(solution)/shard_map/ppermute | solution.py:23
  452.2 7.5 %collective-permute-start.40 = (f32[18,1,128]{2,1,0:T(1,128)S(1)}, f32[18,1,128]{2,1,0:T(1,128)S(1)}, u32[]{:S(2)}, u32[]{:S(2)}) collective-permute-start(f32[18,1,128]{2,1,0:T(1,128)S(1)} %get-tuple-element.34), channel_id=1, source_target_pairs={{1,0},{2,1},{3,2},{4,3},{5,4},{6,5},{7,6},{8,7},{9,8},{10,9},{11,1... | collective-permute-start | bytes 27656 | tf_op jit(solution)/shard_map/ppermute | solution.py:23
  463.7 5.1 %collective-permute-done.41 = f32[18,1,128]{2,1,0:T(1,128)S(1)} collective-permute-done((f32[18,1,128]{2,1,0:T(1,128)S(1)}, f32[18,1,128]{2,1,0:T(1,128)S(1)}, u32[]{:S(2)}, u32[]{:S(2)}) %collective-permute-start.41) | collective-permute-done | bytes 9248 | tf_op jit(solution)/shard_map/ppermute | solution.py:21
  469.0 1.9 collective-permute-start.43
  470.9 5.8 %collective-permute-start.44 = (f32[1,16,128]{2,1,0:T(8,128)S(1)}, f32[1,16,128]{2,1,0:T(8,128)S(1)}, u32[]{:S(2)}, u32[]{:S(2)}) collective-permute-start(f32[1,16,128]{2,1,0:T(8,128)S(1)} %get-tuple-element.23), channel_id=1, source_target_pairs={{16,0},{32,16},{48,32},{64,48},{80,64},{96,80},{112,96},{128,112},... | collective-permute-start | bytes 24584 | tf_op jit(solution)/shard_map/ppermute | solution.py:23
  478.7 5.8 %collective-permute-start.47 = (f32[1,16,128]{2,1,0:T(8,128)S(1)}, f32[1,16,128]{2,1,0:T(8,128)S(1)}, u32[]{:S(2)}, u32[]{:S(2)}) collective-permute-start(f32[1,16,128]{2,1,0:T(8,128)S(1)} %get-tuple-element.45), channel_id=1, source_target_pairs={{16,0},{32,16},{48,32},{64,48},{80,64},{96,80},{112,96},{128,112},... | collective-permute-start | bytes 24584 | tf_op jit(solution)/shard_map/ppermute | solution.py:23
  486.5 7.5 %collective-permute-start.48 = (f32[18,1,128]{2,1,0:T(1,128)S(1)}, f32[18,1,128]{2,1,0:T(1,128)S(1)}, u32[]{:S(2)}, u32[]{:S(2)}) collective-permute-start(f32[18,1,128]{2,1,0:T(1,128)S(1)} %get-tuple-element.32), channel_id=1, source_target_pairs={{1,0},{2,1},{3,2},{4,3},{5,4},{6,5},{7,6},{8,7},{9,8},{10,9},{11,1... | collective-permute-start | bytes 27656 | tf_op jit(solution)/shard_map/ppermute | solution.py:23
  496.1 7.1 %collective-permute-done.49 = f32[18,1,128]{2,1,0:T(1,128)S(1)} collective-permute-done((f32[18,1,128]{2,1,0:T(1,128)S(1)}, f32[18,1,128]{2,1,0:T(1,128)S(1)}, u32[]{:S(2)}, u32[]{:S(2)}) %collective-permute-start.49) | collective-permute-done | bytes 9248 | tf_op jit(solution)/shard_map/ppermute | solution.py:21
  (162 shorter events, 44.3 us)
Async XLA Ops:
  7.2 69.2 %all-gather.2.cloned.1.call-start = ((), (), s32[]{:S(2)}) async-start(), calls=%async_computation.1 | async-start | bytes 1081344 | tf_op jit(solution)/shard_map/all_gather | solution.py:64
  7.9 300.7 %reduce-scatter.2.cloned.1.call-start = ((), (), s32[]{:S(2)}) async-start(), calls=%async_computation.2 | async-start | bytes 2228224 | tf_op jit(solution)/shard_map/reduce_scatter | solution.py:87
  95.3 222.1 %collective-permute-start.4 = (f32[1,16,128]{2,1,0:T(8,128)S(1)}, f32[1,16,128]{2,1,0:T(8,128)S(1)}, u32[]{:S(2)}, u32[]{:S(2)}) collective-permute-start(f32[1,16,128]{2,1,0:T(8,128)S(1)} %broadcast.92), channel_id=1, source_target_pairs={{0,16},{16,32},{32,48},{48,64},{64,80},{80,96},{96,112},{112,128},... | collective-permute-start | bytes 24584 | tf_op jit(solution)/shard_map/ppermute | solution.py:21
  97.4 219.9 %collective-permute-start.5 = (f32[1,16,128]{2,1,0:T(8,128)S(1)}, f32[1,16,128]{2,1,0:T(8,128)S(1)}, u32[]{:S(2)}, u32[]{:S(2)}) collective-permute-start(f32[1,16,128]{2,1,0:T(8,128)S(1)} %broadcast.92), channel_id=1, source_target_pairs={{16,0},{32,16},{48,32},{64,48},{80,64},{96,80},{112,96},{128,112},... | collective-permute-start | bytes 24584 | tf_op jit(solution)/shard_map/ppermute | solution.py:23
  112.1 9.5 %collective-permute-start.2 = (f32[18,1]{1,0:T(8,128)S(1)}, f32[18,1]{1,0:T(8,128)S(1)}, u32[]{:S(2)}, u32[]{:S(2)}) collective-permute-start(f32[18,1]{1,0:T(8,128)S(1)} %get-tuple-element.56), channel_id=1, source_target_pairs={{0,1},{1,2},{2,3},{3,4},{4,5},{5,6},{6,7},{7,8},{8,9},{9,10},{10,1... | collective-permute-start | bytes 224 | tf_op jit(solution)/shard_map/ppermute | solution.py:21
  309.7 10.2 %collective-permute-start.7 = (f32[1,16,128]{2,1,0:T(8,128)S(1)}, f32[1,16,128]{2,1,0:T(8,128)S(1)}, u32[]{:S(2)}, u32[]{:S(2)}) collective-permute-start(f32[1,16,128]{2,1,0:T(8,128)S(1)} %get-tuple-element.55), channel_id=1, source_target_pairs={{0,16},{16,32},{32,48},{48,64},{64,80},{80,96},{96,112},{112,128},... | collective-permute-start | bytes 24584 | tf_op jit(solution)/shard_map/ppermute | solution.py:21
  311.6 8.3 %collective-permute-start.8 = (f32[1,16,128]{2,1,0:T(8,128)S(1)}, f32[1,16,128]{2,1,0:T(8,128)S(1)}, u32[]{:S(2)}, u32[]{:S(2)}) collective-permute-start(f32[1,16,128]{2,1,0:T(8,128)S(1)} %get-tuple-element.54), channel_id=1, source_target_pairs={{16,0},{32,16},{48,32},{64,48},{80,64},{96,80},{112,96},{128,112},... | collective-permute-start | bytes 24584 | tf_op jit(solution)/shard_map/ppermute | solution.py:23
  317.4 14.0 %collective-permute-start.6 = (f32[18,1,128]{2,1,0:T(1,128)S(1)}, f32[18,1,128]{2,1,0:T(1,128)S(1)}, u32[]{:S(2)}, u32[]{:S(2)}) collective-permute-start(f32[18,1,128]{2,1,0:T(1,128)S(1)} %pad_maximum_fusion.83), channel_id=1, source_target_pairs={{0,1},{1,2},{2,3},{3,4},{4,5},{5,6},{6,7},{7,8},{8,9},{9,10},{10,1... | collective-permute-start | bytes 27656 | tf_op jit(solution)/shard_map/ppermute | solution.py:21
  319.9 11.6 %collective-permute-start.10 = (f32[18,1,128]{2,1,0:T(1,128)S(1)}, f32[18,1,128]{2,1,0:T(1,128)S(1)}, u32[]{:S(2)}, u32[]{:S(2)}) collective-permute-start(f32[18,1,128]{2,1,0:T(1,128)S(1)} %get-tuple-element.43), channel_id=1, source_target_pairs={{0,1},{1,2},{2,3},{3,4},{4,5},{5,6},{6,7},{7,8},{8,9},{9,10},{10,1... | collective-permute-start | bytes 27656 | tf_op jit(solution)/shard_map/ppermute | solution.py:21
  329.5 29.6 %collective-permute-start.18 = (f32[1,16,128]{2,1,0:T(8,128)S(1)}, f32[1,16,128]{2,1,0:T(8,128)S(1)}, u32[]{:S(2)}, u32[]{:S(2)}) collective-permute-start(f32[1,16,128]{2,1,0:T(8,128)S(1)} %slice.550), channel_id=1, source_target_pairs={{0,16},{16,32},{32,48},{48,64},{64,80},{80,96},{96,112},{112,128},... | collective-permute-start | bytes 24584 | tf_op jit(solution)/shard_map/ppermute | solution.py:21
  331.6 15.5 %collective-permute-start.11 = (f32[1,16,128]{2,1,0:T(8,128)S(1)}, f32[1,16,128]{2,1,0:T(8,128)S(1)}, u32[]{:S(2)}, u32[]{:S(2)}) collective-permute-start(f32[1,16,128]{2,1,0:T(8,128)S(1)} %get-tuple-element.30), channel_id=1, source_target_pairs={{0,16},{16,32},{32,48},{48,64},{64,80},{80,96},{96,112},{112,128},... | collective-permute-start | bytes 24584 | tf_op jit(solution)/shard_map/ppermute | solution.py:21
  333.6 13.6 %collective-permute-start.12 = (f32[1,16,128]{2,1,0:T(8,128)S(1)}, f32[1,16,128]{2,1,0:T(8,128)S(1)}, u32[]{:S(2)}, u32[]{:S(2)}) collective-permute-start(f32[1,16,128]{2,1,0:T(8,128)S(1)} %get-tuple-element.31), channel_id=1, source_target_pairs={{16,0},{32,16},{48,32},{64,48},{80,64},{96,80},{112,96},{128,112},... | collective-permute-start | bytes 24584 | tf_op jit(solution)/shard_map/ppermute | solution.py:23
  339.5 12.3 %collective-permute-start.14 = (f32[1,16,128]{2,1,0:T(8,128)S(1)}, f32[1,16,128]{2,1,0:T(8,128)S(1)}, u32[]{:S(2)}, u32[]{:S(2)}) collective-permute-start(f32[1,16,128]{2,1,0:T(8,128)S(1)} %get-tuple-element.53), channel_id=1, source_target_pairs={{0,16},{16,32},{32,48},{48,64},{64,80},{80,96},{96,112},{112,128},... | collective-permute-start | bytes 24584 | tf_op jit(solution)/shard_map/ppermute | solution.py:21
  341.4 10.4 %collective-permute-start.15 = (f32[1,16,128]{2,1,0:T(8,128)S(1)}, f32[1,16,128]{2,1,0:T(8,128)S(1)}, u32[]{:S(2)}, u32[]{:S(2)}) collective-permute-start(f32[1,16,128]{2,1,0:T(8,128)S(1)} %get-tuple-element.52), channel_id=1, source_target_pairs={{16,0},{32,16},{48,32},{64,48},{80,64},{96,80},{112,96},{128,112},... | collective-permute-start | bytes 24584 | tf_op jit(solution)/shard_map/ppermute | solution.py:23
  347.2 14.0 %collective-permute-start.13 = (f32[18,1,128]{2,1,0:T(1,128)S(1)}, f32[18,1,128]{2,1,0:T(1,128)S(1)}, u32[]{:S(2)}, u32[]{:S(2)}) collective-permute-start(f32[18,1,128]{2,1,0:T(1,128)S(1)} %pad_maximum_fusion.78), channel_id=1, source_target_pairs={{0,1},{1,2},{2,3},{3,4},{4,5},{5,6},{6,7},{7,8},{8,9},{9,10},{10,1... | collective-permute-start | bytes 27656 | tf_op jit(solution)/shard_map/ppermute | solution.py:21
  351.8 9.5 %collective-permute-start.16 = (f32[18,1,128]{2,1,0:T(1,128)S(1)}, f32[18,1,128]{2,1,0:T(1,128)S(1)}, u32[]{:S(2)}, u32[]{:S(2)}) collective-permute-start(f32[18,1,128]{2,1,0:T(1,128)S(1)} %get-tuple-element.40), channel_id=1, source_target_pairs={{1,0},{2,1},{3,2},{4,3},{5,4},{6,5},{7,6},{8,7},{9,8},{10,9},{11,1... | collective-permute-start | bytes 27656 | tf_op jit(solution)/shard_map/ppermute | solution.py:23
  356.7 9.2 %collective-permute-start.17 = (f32[18,1,128]{2,1,0:T(1,128)S(1)}, f32[18,1,128]{2,1,0:T(1,128)S(1)}, u32[]{:S(2)}, u32[]{:S(2)}) collective-permute-start(f32[18,1,128]{2,1,0:T(1,128)S(1)} %get-tuple-element.41), channel_id=1, source_target_pairs={{0,1},{1,2},{2,3},{3,4},{4,5},{5,6},{6,7},{7,8},{8,9},{9,10},{10,1... | collective-permute-start | bytes 27656 | tf_op jit(solution)/shard_map/ppermute | solution.py:21
  359.3 33.7 %collective-permute-start.26 = (f32[1,16,128]{2,1,0:T(8,128)S(1)}, f32[1,16,128]{2,1,0:T(8,128)S(1)}, u32[]{:S(2)}, u32[]{:S(2)}) collective-permute-start(f32[1,16,128]{2,1,0:T(8,128)S(1)} %slice.561), channel_id=1, source_target_pairs={{0,16},{16,32},{32,48},{48,64},{64,80},{80,96},{96,112},{112,128},... | collective-permute-start | bytes 24584 | tf_op jit(solution)/shard_map/ppermute | solution.py:21
  366.0 15.5 %collective-permute-start.19 = (f32[1,16,128]{2,1,0:T(8,128)S(1)}, f32[1,16,128]{2,1,0:T(8,128)S(1)}, u32[]{:S(2)}, u32[]{:S(2)}) collective-permute-start(f32[1,16,128]{2,1,0:T(8,128)S(1)} %get-tuple-element.28), channel_id=1, source_target_pairs={{0,16},{16,32},{32,48},{48,64},{64,80},{80,96},{96,112},{112,128},... | collective-permute-start | bytes 24584 | tf_op jit(solution)/shard_map/ppermute | solution.py:21
  368.0 13.5 %collective-permute-start.20 = (f32[1,16,128]{2,1,0:T(8,128)S(1)}, f32[1,16,128]{2,1,0:T(8,128)S(1)}, u32[]{:S(2)}, u32[]{:S(2)}) collective-permute-start(f32[1,16,128]{2,1,0:T(8,128)S(1)} %get-tuple-element.29), channel_id=1, source_target_pairs={{16,0},{32,16},{48,32},{64,48},{80,64},{96,80},{112,96},{128,112},... | collective-permute-start | bytes 24584 | tf_op jit(solution)/shard_map/ppermute | solution.py:23
  373.8 9.7 %collective-permute-start.22 = (f32[1,16,128]{2,1,0:T(8,128)S(1)}, f32[1,16,128]{2,1,0:T(8,128)S(1)}, u32[]{:S(2)}, u32[]{:S(2)}) collective-permute-start(f32[1,16,128]{2,1,0:T(8,128)S(1)} %get-tuple-element.51), channel_id=1, source_target_pairs={{0,16},{16,32},{32,48},{48,64},{64,80},{80,96},{96,112},{112,128},... | collective-permute-start | bytes 24584 | tf_op jit(solution)/shard_map/ppermute | solution.py:21
  375.7 7.7 %collective-permute-start.23 = (f32[1,16,128]{2,1,0:T(8,128)S(1)}, f32[1,16,128]{2,1,0:T(8,128)S(1)}, u32[]{:S(2)}, u32[]{:S(2)}) collective-permute-start(f32[1,16,128]{2,1,0:T(8,128)S(1)} %get-tuple-element.50), channel_id=1, source_target_pairs={{16,0},{32,16},{48,32},{64,48},{80,64},{96,80},{112,96},{128,112},... | collective-permute-start | bytes 24584 | tf_op jit(solution)/shard_map/ppermute | solution.py:23
  381.5 13.5 %collective-permute-start.21 = (f32[18,1,128]{2,1,0:T(1,128)S(1)}, f32[18,1,128]{2,1,0:T(1,128)S(1)}, u32[]{:S(2)}, u32[]{:S(2)}) collective-permute-start(f32[18,1,128]{2,1,0:T(1,128)S(1)} %pad_maximum_fusion.73), channel_id=1, source_target_pairs={{0,1},{1,2},{2,3},{3,4},{4,5},{5,6},{6,7},{7,8},{8,9},{9,10},{10,1... | collective-permute-start | bytes 27656 | tf_op jit(solution)/shard_map/ppermute | solution.py:21
  383.5 11.6 %collective-permute-start.24 = (f32[18,1,128]{2,1,0:T(1,128)S(1)}, f32[18,1,128]{2,1,0:T(1,128)S(1)}, u32[]{:S(2)}, u32[]{:S(2)}) collective-permute-start(f32[18,1,128]{2,1,0:T(1,128)S(1)} %get-tuple-element.38), channel_id=1, source_target_pairs={{1,0},{2,1},{3,2},{4,3},{5,4},{6,5},{7,6},{8,7},{9,8},{10,9},{11,1... | collective-permute-start | bytes 27656 | tf_op jit(solution)/shard_map/ppermute | solution.py:23
  391.1 9.2 %collective-permute-start.25 = (f32[18,1,128]{2,1,0:T(1,128)S(1)}, f32[18,1,128]{2,1,0:T(1,128)S(1)}, u32[]{:S(2)}, u32[]{:S(2)}) collective-permute-start(f32[18,1,128]{2,1,0:T(1,128)S(1)} %get-tuple-element.39), channel_id=1, source_target_pairs={{0,1},{1,2},{2,3},{3,4},{4,5},{5,6},{6,7},{7,8},{8,9},{9,10},{10,1... | collective-permute-start | bytes 27656 | tf_op jit(solution)/shard_map/ppermute | solution.py:21
  393.1 34.2 %collective-permute-start.34 = (f32[1,16,128]{2,1,0:T(8,128)S(1)}, f32[1,16,128]{2,1,0:T(8,128)S(1)}, u32[]{:S(2)}, u32[]{:S(2)}) collective-permute-start(f32[1,16,128]{2,1,0:T(8,128)S(1)} %slice.572), channel_id=1, source_target_pairs={{0,16},{16,32},{32,48},{48,64},{64,80},{80,96},{96,112},{112,128},... | collective-permute-start | bytes 24584 | tf_op jit(solution)/shard_map/ppermute | solution.py:21
  400.4 15.5 %collective-permute-start.27 = (f32[1,16,128]{2,1,0:T(8,128)S(1)}, f32[1,16,128]{2,1,0:T(8,128)S(1)}, u32[]{:S(2)}, u32[]{:S(2)}) collective-permute-start(f32[1,16,128]{2,1,0:T(8,128)S(1)} %get-tuple-element.26), channel_id=1, source_target_pairs={{0,16},{16,32},{32,48},{48,64},{64,80},{80,96},{96,112},{112,128},... | collective-permute-start | bytes 24584 | tf_op jit(solution)/shard_map/ppermute | solution.py:21
  402.3 13.5 %collective-permute-start.28 = (f32[1,16,128]{2,1,0:T(8,128)S(1)}, f32[1,16,128]{2,1,0:T(8,128)S(1)}, u32[]{:S(2)}, u32[]{:S(2)}) collective-permute-start(f32[1,16,128]{2,1,0:T(8,128)S(1)} %get-tuple-element.27), channel_id=1, source_target_pairs={{16,0},{32,16},{48,32},{64,48},{80,64},{96,80},{112,96},{128,112},... | collective-permute-start | bytes 24584 | tf_op jit(solution)/shard_map/ppermute | solution.py:23
  408.1 9.7 %collective-permute-start.30 = (f32[1,16,128]{2,1,0:T(8,128)S(1)}, f32[1,16,128]{2,1,0:T(8,128)S(1)}, u32[]{:S(2)}, u32[]{:S(2)}) collective-permute-start(f32[1,16,128]{2,1,0:T(8,128)S(1)} %get-tuple-element.49), channel_id=1, source_target_pairs={{0,16},{16,32},{32,48},{48,64},{64,80},{80,96},{96,112},{112,128},... | collective-permute-start | bytes 24584 | tf_op jit(solution)/shard_map/ppermute | solution.py:21
  410.1 7.7 %collective-permute-start.31 = (f32[1,16,128]{2,1,0:T(8,128)S(1)}, f32[1,16,128]{2,1,0:T(8,128)S(1)}, u32[]{:S(2)}, u32[]{:S(2)}) collective-permute-start(f32[1,16,128]{2,1,0:T(8,128)S(1)} %get-tuple-element.48), channel_id=1, source_target_pairs={{16,0},{32,16},{48,32},{64,48},{80,64},{96,80},{112,96},{128,112},... | collective-permute-start | bytes 24584 | tf_op jit(solution)/shard_map/ppermute | solution.py:23
  415.9 13.5 %collective-permute-start.29 = (f32[18,1,128]{2,1,0:T(1,128)S(1)}, f32[18,1,128]{2,1,0:T(1,128)S(1)}, u32[]{:S(2)}, u32[]{:S(2)}) collective-permute-start(f32[18,1,128]{2,1,0:T(1,128)S(1)} %pad_maximum_fusion.68), channel_id=1, source_target_pairs={{0,1},{1,2},{2,3},{3,4},{4,5},{5,6},{6,7},{7,8},{8,9},{9,10},{10,1... | collective-permute-start | bytes 27656 | tf_op jit(solution)/shard_map/ppermute | solution.py:21
  417.8 11.6 %collective-permute-start.32 = (f32[18,1,128]{2,1,0:T(1,128)S(1)}, f32[18,1,128]{2,1,0:T(1,128)S(1)}, u32[]{:S(2)}, u32[]{:S(2)}) collective-permute-start(f32[18,1,128]{2,1,0:T(1,128)S(1)} %get-tuple-element.36), channel_id=1, source_target_pairs={{1,0},{2,1},{3,2},{4,3},{5,4},{6,5},{7,6},{8,7},{9,8},{10,9},{11,1... | collective-permute-start | bytes 27656 | tf_op jit(solution)/shard_map/ppermute | solution.py:23
  425.4 9.2 %collective-permute-start.33 = (f32[18,1,128]{2,1,0:T(1,128)S(1)}, f32[18,1,128]{2,1,0:T(1,128)S(1)}, u32[]{:S(2)}, u32[]{:S(2)}) collective-permute-start(f32[18,1,128]{2,1,0:T(1,128)S(1)} %get-tuple-element.37), channel_id=1, source_target_pairs={{0,1},{1,2},{2,3},{3,4},{4,5},{5,6},{6,7},{7,8},{8,9},{9,10},{10,1... | collective-permute-start | bytes 27656 | tf_op jit(solution)/shard_map/ppermute | solution.py:21
  427.5 34.2 %collective-permute-start.42 = (f32[1,16,128]{2,1,0:T(8,128)S(1)}, f32[1,16,128]{2,1,0:T(8,128)S(1)}, u32[]{:S(2)}, u32[]{:S(2)}) collective-permute-start(f32[1,16,128]{2,1,0:T(8,128)S(1)} %slice.583), channel_id=1, source_target_pairs={{0,16},{16,32},{32,48},{48,64},{64,80},{80,96},{96,112},{112,128},... | collective-permute-start | bytes 24584 | tf_op jit(solution)/shard_map/ppermute | solution.py:21
  434.7 15.5 %collective-permute-start.35 = (f32[1,16,128]{2,1,0:T(8,128)S(1)}, f32[1,16,128]{2,1,0:T(8,128)S(1)}, u32[]{:S(2)}, u32[]{:S(2)}) collective-permute-start(f32[1,16,128]{2,1,0:T(8,128)S(1)} %get-tuple-element.24), channel_id=1, source_target_pairs={{0,16},{16,32},{32,48},{48,64},{64,80},{80,96},{96,112},{112,128},... | collective-permute-start | bytes 24584 | tf_op jit(solution)/shard_map/ppermute | solution.py:21
  436.6 13.5 %collective-permute-start.36 = (f32[1,16,128]{2,1,0:T(8,128)S(1)}, f32[1,16,128]{2,1,0:T(8,128)S(1)}, u32[]{:S(2)}, u32[]{:S(2)}) collective-permute-start(f32[1,16,128]{2,1,0:T(8,128)S(1)} %get-tuple-element.25), channel_id=1, source_target_pairs={{16,0},{32,16},{48,32},{64,48},{80,64},{96,80},{112,96},{128,112},... | collective-permute-start | bytes 24584 | tf_op jit(solution)/shard_map/ppermute | solution.py:23
  442.5 9.7 %collective-permute-start.38 = (f32[1,16,128]{2,1,0:T(8,128)S(1)}, f32[1,16,128]{2,1,0:T(8,128)S(1)}, u32[]{:S(2)}, u32[]{:S(2)}) collective-permute-start(f32[1,16,128]{2,1,0:T(8,128)S(1)} %get-tuple-element.47), channel_id=1, source_target_pairs={{0,16},{16,32},{32,48},{48,64},{64,80},{80,96},{96,112},{112,128},... | collective-permute-start | bytes 24584 | tf_op jit(solution)/shard_map/ppermute | solution.py:21
  444.4 7.7 %collective-permute-start.39 = (f32[1,16,128]{2,1,0:T(8,128)S(1)}, f32[1,16,128]{2,1,0:T(8,128)S(1)}, u32[]{:S(2)}, u32[]{:S(2)}) collective-permute-start(f32[1,16,128]{2,1,0:T(8,128)S(1)} %get-tuple-element.46), channel_id=1, source_target_pairs={{16,0},{32,16},{48,32},{64,48},{80,64},{96,80},{112,96},{128,112},... | collective-permute-start | bytes 24584 | tf_op jit(solution)/shard_map/ppermute | solution.py:23
  450.2 13.5 %collective-permute-start.37 = (f32[18,1,128]{2,1,0:T(1,128)S(1)}, f32[18,1,128]{2,1,0:T(1,128)S(1)}, u32[]{:S(2)}, u32[]{:S(2)}) collective-permute-start(f32[18,1,128]{2,1,0:T(1,128)S(1)} %pad_maximum_fusion.63), channel_id=1, source_target_pairs={{0,1},{1,2},{2,3},{3,4},{4,5},{5,6},{6,7},{7,8},{8,9},{9,10},{10,1... | collective-permute-start | bytes 27656 | tf_op jit(solution)/shard_map/ppermute | solution.py:21
  452.2 11.6 %collective-permute-start.40 = (f32[18,1,128]{2,1,0:T(1,128)S(1)}, f32[18,1,128]{2,1,0:T(1,128)S(1)}, u32[]{:S(2)}, u32[]{:S(2)}) collective-permute-start(f32[18,1,128]{2,1,0:T(1,128)S(1)} %get-tuple-element.34), channel_id=1, source_target_pairs={{1,0},{2,1},{3,2},{4,3},{5,4},{6,5},{7,6},{8,7},{9,8},{10,9},{11,1... | collective-permute-start | bytes 27656 | tf_op jit(solution)/shard_map/ppermute | solution.py:23
  459.7 9.2 %collective-permute-start.41 = (f32[18,1,128]{2,1,0:T(1,128)S(1)}, f32[18,1,128]{2,1,0:T(1,128)S(1)}, u32[]{:S(2)}, u32[]{:S(2)}) collective-permute-start(f32[18,1,128]{2,1,0:T(1,128)S(1)} %get-tuple-element.35), channel_id=1, source_target_pairs={{0,1},{1,2},{2,3},{3,4},{4,5},{5,6},{6,7},{7,8},{8,9},{9,10},{10,1... | collective-permute-start | bytes 27656 | tf_op jit(solution)/shard_map/ppermute | solution.py:21
  461.8 34.2 %collective-permute-start.50 = (f32[1,16,128]{2,1,0:T(8,128)S(1)}, f32[1,16,128]{2,1,0:T(8,128)S(1)}, u32[]{:S(2)}, u32[]{:S(2)}) collective-permute-start(f32[1,16,128]{2,1,0:T(8,128)S(1)} %slice.594), channel_id=1, source_target_pairs={{0,16},{16,32},{32,48},{48,64},{64,80},{80,96},{96,112},{112,128},... | collective-permute-start | bytes 24584 | tf_op jit(solution)/shard_map/ppermute | solution.py:21
  469.0 15.5 %collective-permute-start.43 = (f32[1,16,128]{2,1,0:T(8,128)S(1)}, f32[1,16,128]{2,1,0:T(8,128)S(1)}, u32[]{:S(2)}, u32[]{:S(2)}) collective-permute-start(f32[1,16,128]{2,1,0:T(8,128)S(1)} %get-tuple-element.22), channel_id=1, source_target_pairs={{0,16},{16,32},{32,48},{48,64},{64,80},{80,96},{96,112},{112,128},... | collective-permute-start | bytes 24584 | tf_op jit(solution)/shard_map/ppermute | solution.py:21
  470.9 13.5 %collective-permute-start.44 = (f32[1,16,128]{2,1,0:T(8,128)S(1)}, f32[1,16,128]{2,1,0:T(8,128)S(1)}, u32[]{:S(2)}, u32[]{:S(2)}) collective-permute-start(f32[1,16,128]{2,1,0:T(8,128)S(1)} %get-tuple-element.23), channel_id=1, source_target_pairs={{16,0},{32,16},{48,32},{64,48},{80,64},{96,80},{112,96},{128,112},... | collective-permute-start | bytes 24584 | tf_op jit(solution)/shard_map/ppermute | solution.py:23
  476.8 9.7 %collective-permute-start.46 = (f32[1,16,128]{2,1,0:T(8,128)S(1)}, f32[1,16,128]{2,1,0:T(8,128)S(1)}, u32[]{:S(2)}, u32[]{:S(2)}) collective-permute-start(f32[1,16,128]{2,1,0:T(8,128)S(1)} %get-tuple-element.44), channel_id=1, source_target_pairs={{0,16},{16,32},{32,48},{48,64},{64,80},{80,96},{96,112},{112,128},... | collective-permute-start | bytes 24584 | tf_op jit(solution)/shard_map/ppermute | solution.py:21
  484.5 11.6 %collective-permute-start.45 = (f32[18,1,128]{2,1,0:T(1,128)S(1)}, f32[18,1,128]{2,1,0:T(1,128)S(1)}, u32[]{:S(2)}, u32[]{:S(2)}) collective-permute-start(f32[18,1,128]{2,1,0:T(1,128)S(1)} %pad_maximum_fusion.58), channel_id=1, source_target_pairs={{0,1},{1,2},{2,3},{3,4},{4,5},{5,6},{6,7},{7,8},{8,9},{9,10},{10,1... | collective-permute-start | bytes 27656 | tf_op jit(solution)/shard_map/ppermute | solution.py:21
  486.5 9.6 %collective-permute-start.48 = (f32[18,1,128]{2,1,0:T(1,128)S(1)}, f32[18,1,128]{2,1,0:T(1,128)S(1)}, u32[]{:S(2)}, u32[]{:S(2)}) collective-permute-start(f32[18,1,128]{2,1,0:T(1,128)S(1)} %get-tuple-element.32), channel_id=1, source_target_pairs={{1,0},{2,1},{3,2},{4,3},{5,4},{6,5},{7,6},{8,7},{9,8},{10,9},{11,1... | collective-permute-start | bytes 27656 | tf_op jit(solution)/shard_map/ppermute | solution.py:23
  494.0 9.2 %collective-permute-start.49 = (f32[18,1,128]{2,1,0:T(1,128)S(1)}, f32[18,1,128]{2,1,0:T(1,128)S(1)}, u32[]{:S(2)}, u32[]{:S(2)}) collective-permute-start(f32[18,1,128]{2,1,0:T(1,128)S(1)} %get-tuple-element.33), channel_id=1, source_target_pairs={{0,1},{1,2},{2,3},{3,4},{4,5},{5,6},{6,7},{7,8},{8,9},{9,10},{10,1... | collective-permute-start | bytes 27656 | tf_op jit(solution)/shard_map/ppermute | solution.py:21
  (16 other events, 248.5 us)
Sparse Core Ops, SparseCore 0:
  10.2 66.1 all-gather.1
  95.4 213.1 reduce-scatter.1
where the time goes:
time: 513 us; the launch traced here: 511 us
  waiting for transfers between devices  283 us (55%)
  starting transfers between devices  188 us (37%)
  between operations  15.3 us (3%)
  local copies, waits for them, and re-layouts  9.79 us (2%)
  matrix products  9.23 us (2%)
  other arithmetic  5.81 us (1%)
    reduce_scatter x1, waiting for transfers between devices, on_device(): summed = lax.psum_scatter(ordered, 'fault', scatter_dimension=0, tiled=True)  184 us
    ppermute x20, starting transfers between devices, extended(): lax.ppermute(head, axis, [((i + 1) % count, i) for i in range(ends)])  120 us
    ppermute x31, starting transfers between devices, extended(): lax.ppermute(tail, axis, [(i, (i + 1) % count) for i in range(ends)])  68.3 us
    all_gather x1, waiting for transfers between devices, on_device(): gathered = lax.all_gather(slip_rate, 'sea', axis=0, tiled=True)  66.4 us
    ppermute x31, waiting for transfers between devices, extended(): lax.ppermute(tail, axis, [(i, (i + 1) % count) for i in range(ends)])  27.2 us
  transfers between devices with their start and end apart: 53, of which 9 were waited for; matrix products, arithmetic and copies ran while one was open for 1% of the time, Pallas kernels for 0%

commit v1 on v0

v1 whole, which is shorter than its diff:
```python
import jax
import jax.numpy as jnp
from jax import lax
from jax.experimental import pallas as pl
from jax.experimental.pallas import tpu as pltpu
from jax.sharding import PartitionSpec as P

STEPS = 6
GRAVITY_STEP = 0.7
HEIGHT_STEP = 0.7
GAIN = GRAVITY_STEP * HEIGHT_STEP
MESH = pl.DeviceIdType.MESH
F32, BF16 = jnp.float32, jnp.bfloat16

SEA, FAULT = 32, 16
LEAF, MEMBERS, RANK = 256, 128, 48
NEAR, FAR, LEAVES = 8, 24, 16
BRICK = 16
ROWS, COLS = BRICK + 2 * STEPS, BRICK + 16
TOP, LEFT = STEPS, 8
NEIGHBOURS = [(dy, dx) for dy in (-1, 0, 1) for dx in (-1, 0, 1) if (dy, dx) != (0, 0)]
RING = (1, 7, 2, 6, 3, 5, 4)
GROUP = 4


def mod(a, n):
    return lax.rem(a + n, n)


def kernel(
    slip, near_hbm, near_rows, near_cols, near_scale, left_hbm, right_hbm, far_rows, far_cols, far_rank, far_scale, depth, wet,
    uplift, level,
    slips, near, left, right, coeffs, acc, chain, last, x_out, x_in, z_out, z_in, depths, compact, wets, east, north, h, e, n,
    load_sem, y_send, y_recv, x_send, x_recv, c_send, c_recv, k_send, k_recv, d_send, d_recv,
    p_send, p_recv, z_send, z_recv, h_send, h_recv,
):
    s, f = lax.axis_index("sea"), lax.axis_index("fault")
    y, x_lo, core = s // 4, (s // 2) % 2, s % 2
    z, x_hi = f // 2, f % 2
    core_mate, x_mate = s + 1 - 2 * core, s + 2 - 4 * x_lo
    far_mate = f + 1 - 2 * x_hi

    def copy(src, dst, send, recv, to_sea, to_fault):
        return pltpu.make_async_remote_copy(
            src_ref=src, dst_ref=dst, send_sem=send, recv_sem=recv, device_id=(to_sea, to_fault), device_id_type=MESH
        )

    barrier = pltpu.get_barrier_semaphore()
    partners = [(mod(s + 4 * d, SEA), f) for d in RING]
    partners += [(core_mate, f), (x_mate, f), (s, far_mate)]
    partners += [(s, mod(f + 2 * d, FAULT)) for d in RING]
    partners += [(mod(s + dy, SEA), mod(f + dx, FAULT)) for dy, dx in NEIGHBOURS]
    for partner in partners:
        pl.semaphore_signal(barrier, inc=1, device_id=partner, device_id_type=MESH)
    loads = [
        pltpu.make_async_copy(src.at[0, 0], dst, load_sem.at[i])
        for i, (src, dst) in enumerate(((right_hbm, right), (near_hbm, near), (left_hbm, left)))
    ]
    for load in loads:
        load.start()
    pl.semaphore_wait(barrier, len(partners))

    def slot(index):
        return slips.at[index // 2, pl.ds(pl.multiple_of((index % 2) * 128, 128), 128), :]

    def along_y(d, back):
        return copy(slip, slot(mod(s - 4 * d, SEA) if back else s), y_send.at[d], y_recv.at[d], mod(s + 4 * d, SEA), f)

    def to_mate(d, mate, send, recv, back):
        mine = mod(s - 4 * d, SEA)
        theirs = mod(mate - 4 * d, SEA)
        src = slip if d == 0 else slot(mine)
        return copy(src, slot(theirs if back else mine), send.at[d], recv.at[d], mate, f)

    def onward(d, back):
        mine = mod(x_mate - 4 * d, SEA)
        theirs = mod(s + 1 - 2 * core + 2 - 4 * x_lo - 4 * d, SEA)
        return copy(slot(mine), slot(theirs if back else mine), k_send.at[d], k_recv.at[d], core_mate, f)

    for d in RING:
        along_y(d, False).start()
    to_mate(0, x_mate, x_send, x_recv, False).start()
    to_mate(0, core_mate, c_send, c_recv, False).start()
    slips[s // 2, pl.ds(pl.multiple_of((s % 2) * 128, 128), 128), :] = slip[...]

    wet_here = wet[...].astype(F32)
    depths[4] = jnp.zeros((BRICK, 128), F32)
    depths[4, :, :BRICK] = depth[...] * wet_here

    def depth_copy(i):
        dy, dx = NEIGHBOURS[i]
        k = (dy + 1) * 3 + dx + 1
        return copy(depths.at[4], depths.at[k], d_send.at[i], d_recv.at[i], mod(s - dy, SEA), mod(f - dx, FAULT))

    for i in range(8):
        depth_copy(i).start()

    acc[0] = jnp.zeros((LEAF, MEMBERS), F32)
    for r in range(LEAVES):
        last[r] = 0

    def link(rows, first):
        def body(b, carry):
            row = rows[0, 0, b]
            chain[first + b] = last[row]
            for r in range(LEAVES):
                last[r] = jnp.where(row == r, first + b, last[r])
            return carry

        return body

    lax.fori_loop(0, NEAR, link(near_rows, 1), 0)
    lax.fori_loop(0, FAR, link(far_rows, 1 + NEAR), 0)

    before = 0
    for d in RING:
        along_y(d, True).wait_recv()
        to_mate(d, x_mate, x_send, x_recv, False).start()
        to_mate(d, core_mate, c_send, c_recv, False).start()
        to_mate(before, x_mate, x_send, x_recv, True).wait_recv()
        onward(before, False).start()
        before = d
    to_mate(before, x_mate, x_send, x_recv, True).wait_recv()
    onward(before, False).start()

    lane = lax.broadcasted_iota(jnp.int32, (BRICK, 128), 1)
    for i in range(8):
        depth_copy(i).wait_recv()
    west_ok, east_ok = f > 0, f < FAULT - 1
    for dy, place in ((-1, 0), (0, TOP), (1, TOP + BRICK)):
        row_ok = (s + dy >= 0) & (s + dy < SEA)
        k = (dy + 1) * 3
        west = jnp.where((lane >= 8) & (lane < 16) & west_ok, depths[k], 0.0)
        east_side = jnp.where((lane < 8) & east_ok, depths[k + 2], 0.0)
        band = pltpu.roll(west, 120, 1) + pltpu.roll(depths[k + 1], 8, 1) + pltpu.roll(east_side, 24, 1)
        band = jnp.where(row_ok, band, 0.0)
        rows = band[BRICK - STEPS :] if dy < 0 else band[:STEPS] if dy > 0 else band
        compact[place : place + rows.shape[0], :] = rows
    eye = lax.broadcasted_iota(jnp.int32, (COLS, 128), 1) == lax.broadcasted_iota(jnp.int32, (COLS, 128), 0)

    def spread(row, width):
        kept = jnp.where(eye[:width], jnp.broadcast_to(row, (width, 128)), 0.0)
        return jnp.broadcast_to(jnp.sum(kept, axis=1, keepdims=True), (width, 128))

    def edges(i, carry):
        here = compact[pl.ds(i, 1), :]
        east[i] = spread(GAIN * jnp.minimum(here, pltpu.roll(here, 127, 1)), COLS)
        north[i] = spread(GAIN * jnp.minimum(here, compact[pl.ds(i + 1, 1), :]), COLS)
        return carry

    compact[ROWS:, :] = jnp.zeros((compact.shape[0] - ROWS, 128), F32)
    lax.fori_loop(0, ROWS, edges, 0)
    depths[9] = jnp.zeros((BRICK, 128), F32)
    depths[9, :, :BRICK] = wet_here

    def dry(i, carry):
        wets[i] = spread(depths[9, pl.ds(i, 1), :], BRICK)
        return carry

    for i in range(8):
        depth_copy(i).wait_send()
    lax.fori_loop(0, BRICK, dry, 0)

    for load in loads:
        load.wait()
    for d in (0,) + RING:
        to_mate(d, core_mate, c_send, c_recv, True).wait_recv()
        onward(d, True).wait_recv()

    rank_of = lax.broadcasted_iota(jnp.int32, (RANK, MEMBERS), 0)

    def project(g, carry):
        for i in range(GROUP):
            b = g * GROUP + i
            made = jnp.dot(right[b], slips[far_cols[0, 0, b]], preferred_element_type=F32)
            coeffs[b] = jnp.where(rank_of < far_rank[0, 0, b], made, 0.0).astype(BF16)
        return carry

    def near_sum(g, carry):
        for i in range(GROUP):
            b = g * GROUP + i
            term = jnp.dot(near[b], slips[near_cols[0, 0, b]], preferred_element_type=F32)
            acc[1 + b] = term * near_scale[0, 0, b] + acc[chain[1 + b]]
        return carry

    def far_sum(g, carry):
        for i in range(GROUP):
            b = g * GROUP + i
            term = lax.dot_general(left[b], coeffs[b], (((0,), (0,)), ((), ())), preferred_element_type=F32)
            acc[1 + NEAR + b] = term * far_scale[0, 0, b] + acc[chain[1 + NEAR + b]]
        return carry

    lax.fori_loop(0, FAR // GROUP, project, 0)
    lax.fori_loop(0, NEAR // GROUP, near_sum, 0)
    lax.fori_loop(0, FAR // GROUP, far_sum, 0)

    def offset(j):
        return 4 + ((j + 1) // 2) * (1 - 2 * (j % 2))

    def part(j, half, r):
        owner = 2 * mod(z + offset(j), 8) + half
        return acc[last[r], pl.ds(pl.multiple_of(owner * BRICK, BRICK), BRICK), :]

    def pair(j):
        return copy(x_out.at[j], x_in.at[j], p_send.at[j], p_recv.at[j], s, far_mate)

    def along_z(j):
        return copy(z_out.at[j], z_in.at[j], z_send.at[j], z_recv.at[j], s, 2 * mod(z + offset(j), 8) + x_hi)

    def send_pair(j, carry):
        for r in range(BRICK):
            x_out[j, r] = part(j, 1 - x_hi, r).astype(BF16)
        pair(j).start()
        return carry

    def send_z(j, carry):
        pair(j).wait_recv()
        for r in range(BRICK):
            z_out[j, r] = (part(j, x_hi, r) + x_in[j, r].astype(F32)).astype(BF16)
        along_z(j).start()
        return carry

    def add_z(j, carry):
        along_z(j).wait_recv()
        for r in range(BRICK):
            uplift[r] = uplift[r] + z_in[j, r].astype(F32)
        return carry

    lax.fori_loop(0, 8, send_pair, 0)
    lax.fori_loop(0, 7, send_z, 0)
    pair(7).wait_recv()
    for r in range(BRICK):
        uplift[r] = part(7, x_hi, r) + x_in[7, r].astype(F32)
    lax.fori_loop(0, 7, add_z, 0)
    for r in range(BRICK):
        h[TOP + r, LEFT : LEFT + BRICK, :] = uplift[r] * wets[r]

    def halo(i):
        dy, dx = NEIGHBOURS[i]
        tall, wide = (BRICK if dy == 0 else STEPS), (BRICK if dx == 0 else 8)
        src_y, dst_y = {-1: (TOP + BRICK - STEPS, 0), 0: (TOP, TOP), 1: (TOP, TOP + BRICK)}[dy]
        src_x, dst_x = {-1: (LEFT + BRICK - 8, 0), 0: (LEFT, LEFT), 1: (LEFT, LEFT + BRICK)}[dx]
        return copy(
            h.at[src_y : src_y + tall, src_x : src_x + wide, :],
            h.at[dst_y : dst_y + tall, dst_x : dst_x + wide, :],
            h_send.at[i], h_recv.at[i], mod(s - dy, SEA), mod(f - dx, FAULT),
        )

    for i in range(8):
        halo(i).start()
    e[...] = jnp.zeros(e.shape, F32)
    n[...] = jnp.zeros(n.shape, F32)
    for d in RING:
        along_y(d, False).wait_send()
    for d in (0,) + RING:
        to_mate(d, x_mate, x_send, x_recv, False).wait_send()
        to_mate(d, core_mate, c_send, c_recv, False).wait_send()
        onward(d, False).wait_send()
    for j in range(8):
        pair(j).wait_send()
    for j in range(7):
        along_z(j).wait_send()
    for i in range(8):
        halo(i).wait()

    for step in range(STEPS):

        def row(i, below):
            here = h[i]
            flow_n = n[i] + (h[i + 1] - here)
            flow_e = e[i] + (pltpu.roll(here, COLS - 1, 0) - here)
            n[i] = flow_n
            e[i] = flow_e
            flux_n = north[i] * flow_n
            flux_e = east[i] * flow_e
            h[i] = here + (flux_e - pltpu.roll(flux_e, 1, 0) + flux_n - below)
            return flux_n

        def first(i):
            flow_n = n[i] + (h[i + 1] - h[i])
            n[i] = flow_n
            return north[i] * flow_n

        lax.fori_loop(step + 1, ROWS - 1 - step, row, first(step))
    level[...] = h[TOP : TOP + BRICK, LEFT : LEFT + BRICK, :]


def on_device(*args):
    vmem = pl.BlockSpec(memory_space=pltpu.VMEM)
    smem = pl.BlockSpec(memory_space=pltpu.SMEM)
    hbm = pl.BlockSpec(memory_space=pl.ANY)
    field = pltpu.VMEM((ROWS, COLS, MEMBERS), F32)
    dma = pltpu.SemaphoreType.DMA
    brick = jax.ShapeDtypeStruct((BRICK, BRICK, MEMBERS), F32)
    return pl.pallas_call(
        kernel,
        out_shape=(brick, brick),
        in_specs=[vmem, hbm, smem, smem, smem, hbm, hbm, smem, smem, smem, smem, vmem, vmem],
        out_specs=(vmem, vmem),
        scratch_shapes=[
            pltpu.VMEM((LEAVES, LEAF, MEMBERS), BF16),
            pltpu.VMEM((NEAR, LEAF, LEAF), BF16),
            pltpu.VMEM((FAR, RANK, LEAF), BF16),
            pltpu.VMEM((FAR, RANK, LEAF), BF16),
            pltpu.VMEM((FAR, RANK, MEMBERS), BF16),
            pltpu.VMEM((1 + NEAR + FAR, LEAF, MEMBERS), F32),
            pltpu.SMEM((1 + NEAR + FAR,), jnp.int32),
            pltpu.SMEM((LEAVES,), jnp.int32),
            pltpu.VMEM((8, BRICK, BRICK, MEMBERS), BF16),
            pltpu.VMEM((8, BRICK, BRICK, MEMBERS), BF16),
            pltpu.VMEM((7, BRICK, BRICK, MEMBERS), BF16),
            pltpu.VMEM((7, BRICK, BRICK, MEMBERS), BF16),
            pltpu.VMEM((10, BRICK, 128), F32),
            pltpu.VMEM((32, 128), F32),
            pltpu.VMEM((BRICK, BRICK, MEMBERS), F32),
            field, field, field, field, field,
            dma((3,)),
            dma((8,)), dma((8,)), dma((8,)), dma((8,)), dma((8,)), dma((8,)), dma((8,)), dma((8,)),
            dma((8,)), dma((8,)),
            dma((8,)), dma((8,)), dma((7,)), dma((7,)), dma((8,)), dma((8,)),
        ],
        compiler_params=pltpu.CompilerParams(
            collective_id=0, has_side_effects=True, vmem_limit_bytes=48 * 2**20
        ),
        name="forecast",
    )(*args)


def solution(mesh):
    blocks = P("sea", "fault", None, None, None)
    lists = P("sea", "fault", None)
    cells = P("sea", "fault")
    return jax.shard_map(
        on_device,
        mesh=mesh,
        in_specs=(
            P(("fault", "sea"), None), blocks, lists, lists, lists, blocks, blocks, lists, lists, lists, lists, cells, cells,
        ),
        out_specs=(lists, lists),
        check_vma=False,
    )
```

time: 513 us -> 76.3 us (0.15)
  the two profiles are of different devices: /device:TPU:288 before, /device:TPU:1 now
where the time goes in v1:
time: 76.3 us; the launch traced here: 75.5 us
  Pallas kernels  63.4 us (83%)
  local copies, waits for them, and re-layouts  11.4 us (15%)
    pallas_call x1, Pallas kernels, on_device(): pl.pallas_call(kernel, out_shape=(brick, brick), in_specs=[vmem, hbm, sme...  63.4 us
    unnamed x28, local copies, waits for them, and re-layouts  11.4 us

profile of v1, /device:TPU:1, one launch (start us, length us, event | category | flops | bytes accessed | tf_op | source)
XLA Modules:
  0.0 75.5 jit_solution(1871629384203582884)
XLA Ops:
  0.6 0.0 copy-start
  0.6 1.2 %copy-done = bf16[1,1,8,256,256]{4,3,2,1,0:T(8,128)(2,1)S(1)} copy-done((bf16[1,1,8,256,256]{4,3,2,1,0:T(8,128)(2,1)S(1)}, bf16[1,1,8,256,256]{4,3,2,1,0:T(8,128)(2,1)}, u32[]{:S(2)}) %copy-start) | copy-done | bytes 1048600
  1.9 0.0 copy-start.1
  1.9 1.1 %copy-done.1 = bf16[1,1,24,48,256]{4,3,2,1,0:T(8,128)(2,1)S(1)} copy-done((bf16[1,1,24,48,256]{4,3,2,1,0:T(8,128)(2,1)S(1)}, bf16[1,1,24,48,256]{4,3,2,1,0:T(8,128)(2,1)}, u32[]{:S(2)}) %copy-start.1) | copy-done | bytes 589848
  2.9 0.0 copy-start.2
  2.9 1.1 %copy-done.2 = bf16[1,1,24,48,256]{4,3,2,1,0:T(8,128)(2,1)S(1)} copy-done((bf16[1,1,24,48,256]{4,3,2,1,0:T(8,128)(2,1)S(1)}, bf16[1,1,24,48,256]{4,3,2,1,0:T(8,128)(2,1)}, u32[]{:S(2)}) %copy-start.2) | copy-done | bytes 589848
  4.0 0.0 copy-start.3
  4.0 0.8 %copy-done.3 = bf16[128,128]{1,0:T(8,128)(2,1)S(1)} copy-done((bf16[128,128]{1,0:T(8,128)(2,1)S(1)}, bf16[128,128]{1,0:T(8,128)(2,1)}, u32[]{:S(2)}) %copy-start.3) | copy-done | bytes 32792
  4.7 0.0 copy-start.4
  4.8 0.7 copy-done.4
  5.4 0.0 copy-start.5
  5.4 0.7 copy-done.5
  6.1 0.0 copy-start.6
  6.1 0.7 copy-done.6
  6.8 0.0 copy-start.7
  6.8 0.7 copy-done.7
  7.5 0.0 copy-start.8
  7.5 0.7 copy-done.8
  8.1 0.0 copy-start.9
  8.1 0.7 copy-done.9
  8.8 0.0 copy-start.10
  8.8 0.7 copy-done.10
  9.4 0.0 copy-start.11
  9.4 0.7 copy-done.11
  10.1 0.0 copy-start.12
  10.1 0.7 copy-done.12
  10.7 63.4 %forecast.1 = (f32[16,16,128]{2,1,0:T(8,128)S(1)}, f32[16,16,128]{2,1,0:T(8,128)S(1)}) custom-call(bf16[128,128]{1,0:T(8,128)(2,1)S(1)} %copy-done.3, bf16[1,1,8,256,256]{4,3,2,1,0:T(8,128)(2,1)S(1)} %copy-done, s32[1,1,8]{2,1,0:T(1,128)S(1)} %copy-done.6, s32[1,1,8]{2,1,0:T(1,128)S(1)} %copy-done.7, f32[1,1,8]{2,1,0:T(1,128)S(1)} %copy-done.8, ...), custom_call_target="tpu_custom_call" | custom-call | tf_op jit(solution)/shard_map/forecast/pallas_call | solution.py:295
  74.1 0.7 copy.17
  74.8 0.7 copy.18
Async XLA Ops:
  0.6 1.2 %copy-start = (bf16[1,1,8,256,256]{4,3,2,1,0:T(8,128)(2,1)S(1)}, bf16[1,1,8,256,256]{4,3,2,1,0:T(8,128)(2,1)}, u32[]{:S(2)}) copy-start(bf16[1,1,8,256,256]{4,3,2,1,0:T(8,128)(2,1)} %near_hbm.1) | copy-start | bytes 3145732
  1.9 1.1 %copy-start.1 = (bf16[1,1,24,48,256]{4,3,2,1,0:T(8,128)(2,1)S(1)}, bf16[1,1,24,48,256]{4,3,2,1,0:T(8,128)(2,1)}, u32[]{:S(2)}) copy-start(bf16[1,1,24,48,256]{4,3,2,1,0:T(8,128)(2,1)} %left_hbm.1) | copy-start | bytes 1769476
  2.9 1.1 %copy-start.2 = (bf16[1,1,24,48,256]{4,3,2,1,0:T(8,128)(2,1)S(1)}, bf16[1,1,24,48,256]{4,3,2,1,0:T(8,128)(2,1)}, u32[]{:S(2)}) copy-start(bf16[1,1,24,48,256]{4,3,2,1,0:T(8,128)(2,1)} %right_hbm.1) | copy-start | bytes 1769476
  4.0 0.8 %copy-start.3 = (bf16[128,128]{1,0:T(8,128)(2,1)S(1)}, bf16[128,128]{1,0:T(8,128)(2,1)}, u32[]{:S(2)}) copy-start(bf16[128,128]{1,0:T(8,128)(2,1)} %slip.1) | copy-start | bytes 98308
  4.7 0.7 copy-start.4
  5.4 0.7 copy-start.5
  6.1 0.7 copy-start.6
  6.8 0.7 copy-start.7
  7.5 0.7 copy-start.8
  8.1 0.7 copy-start.9
  8.8 0.7 copy-start.10
  9.4 0.7 copy-start.11
  10.1 0.7 copy-start.12

commit v2 on v1

v2 whole, which is shorter than its diff:
```python
import jax
import jax.numpy as jnp
from jax import lax
from jax.experimental import pallas as pl
from jax.experimental.pallas import tpu as pltpu
from jax.sharding import PartitionSpec as P

STEPS = 6
GRAVITY_STEP = 0.7
HEIGHT_STEP = 0.7
GAIN = GRAVITY_STEP * HEIGHT_STEP
MESH = pl.DeviceIdType.MESH
F32, BF16 = jnp.float32, jnp.bfloat16

SEA, FAULT = 32, 16
LEAF, MEMBERS, RANK = 256, 128, 48
NEAR, FAR, LEAVES = 8, 24, 16
BRICK = 16
ROWS, COLS = BRICK + 2 * STEPS, BRICK + 16
TOP, LEFT = STEPS, 8
NEIGHBOURS = [(dy, dx) for dy in (-1, 0, 1) for dx in (-1, 0, 1) if (dy, dx) != (0, 0)]
RING = (1, 7, 2, 6, 3, 5, 4)
GROUP = 8
FAR_GROUP = 24
DIRECT = (4,)
LAG = 4


def mod(a, n):
    return lax.rem(a + n, n)


def kernel(
    slip_hbm, near_hbm, near_rows_hbm, near_cols_hbm, near_scale_hbm, left_hbm, right_hbm, far_rows_hbm, far_cols_hbm,
    far_rank_hbm, far_scale_hbm, depth_hbm, wet_hbm,
    both_hbm,
    uplift, slip, near_rows, near_cols, near_scale, far_rows, far_cols, far_rank, far_scale, depth, wet,
    slips, near, left, right, coeffs, acc, chain, last, x_out, x_in, z_out, z_in, depths, compact, wets, strip_out, strip_in, east, north, h, e, n,
    load_sem, y_send, y_recv, x_send, x_recv, c_send, c_recv, k_send, k_recv, d_send, d_recv,
    p_send, p_recv, z_send, z_recv, h_send, h_recv, out_sem,
):
    s, f = lax.axis_index("sea"), lax.axis_index("fault")
    y, x_lo, core = s // 4, (s // 2) % 2, s % 2
    z, x_hi = f // 2, f % 2
    core_mate, x_mate = s + 1 - 2 * core, s + 2 - 4 * x_lo
    far_mate = f + 1 - 2 * x_hi

    def copy(src, dst, send, recv, to_sea, to_fault):
        return pltpu.make_async_remote_copy(
            src_ref=src, dst_ref=dst, send_sem=send, recv_sem=recv, device_id=(to_sea, to_fault), device_id_type=MESH
        )

    barrier = pltpu.get_barrier_semaphore()
    partners = [(mod(s + 4 * d, SEA), f) for d in RING]
    partners += [(mod(x_mate + 4 * d, SEA), f) for d in DIRECT]
    partners += [(core_mate, f), (x_mate, f), (s, far_mate)]
    partners += [(s, mod(f + 2 * d, FAULT)) for d in RING]
    partners += [(mod(s + dy, SEA), mod(f + dx, FAULT)) for dy, dx in NEIGHBOURS]
    for partner in partners:
        pl.semaphore_signal(barrier, inc=1, device_id=partner, device_id_type=MESH)
    pairs = (
        (slip_hbm, slip), (depth_hbm, depth), (wet_hbm, wet), (near_rows_hbm, near_rows), (far_rows_hbm, far_rows),
        (near_cols_hbm, near_cols), (far_cols_hbm, far_cols), (far_rank_hbm, far_rank),
        (near_scale_hbm, near_scale), (far_scale_hbm, far_scale),
        (right_hbm.at[0, 0], right), (near_hbm.at[0, 0], near), (left_hbm.at[0, 0], left),
    )
    loads = [pltpu.make_async_copy(src, dst, load_sem.at[i]) for i, (src, dst) in enumerate(pairs)]
    for load in loads:
        load.start()
    for load in loads[:3]:
        load.wait()
    pl.semaphore_wait(barrier, len(partners))

    def slot(index):
        return slips.at[index // 2, pl.ds(pl.multiple_of((index % 2) * 128, 128), 128), :]

    def along_y(d, back):
        return copy(slip, slot(mod(s - 4 * d, SEA) if back else s), y_send.at[d], y_recv.at[d], mod(s + 4 * d, SEA), f)

    def to_mate(d, mate, send, recv, back):
        mine = mod(s - 4 * d, SEA)
        theirs = mod(mate - 4 * d, SEA)
        src = slip if d == 0 else slot(mine)
        return copy(src, slot(theirs if back else mine), send.at[d], recv.at[d], mate, f)

    def across(d):
        return copy(slip, slot(s), x_send.at[d], x_recv.at[d], mod(x_mate + 4 * d, SEA), f)

    def onward(d, back):
        mine = mod(x_mate - 4 * d, SEA)
        theirs = mod(s + 1 - 2 * core + 2 - 4 * x_lo - 4 * d, SEA)
        return copy(slot(mine), slot(theirs if back else mine), k_send.at[d], k_recv.at[d], core_mate, f)

    for d in RING:
        along_y(d, False).start()
        if d in DIRECT:
            across(d).start()
    to_mate(0, x_mate, x_send, x_recv, False).start()
    to_mate(0, core_mate, c_send, c_recv, False).start()
    slips[s // 2, pl.ds(pl.multiple_of((s % 2) * 128, 128), 128), :] = slip[...]

    wet_here = wet[...].astype(F32)
    depths[4] = jnp.zeros((BRICK, 128), F32)
    depths[4, :, :BRICK] = depth[...] * wet_here

    def depth_copy(i):
        dy, dx = NEIGHBOURS[i]
        k = (dy + 1) * 3 + dx + 1
        return copy(depths.at[4], depths.at[k], d_send.at[i], d_recv.at[i], mod(s - dy, SEA), mod(f - dx, FAULT))

    for i in range(8):
        depth_copy(i).start()

    acc[0] = jnp.zeros((LEAF, MEMBERS), F32)
    for r in range(LEAVES):
        last[r] = 0

    def link(rows, first):
        def body(b, carry):
            row = rows[0, 0, b]
            chain[first + b] = last[row]
            for r in range(LEAVES):
                last[r] = jnp.where(row == r, first + b, last[r])
            return carry

        return body

    for load in loads[3:10]:
        load.wait()
    lax.fori_loop(0, NEAR, link(near_rows, 1), 0)
    lax.fori_loop(0, FAR, link(far_rows, 1 + NEAR), 0)

    def ready(d):
        to_mate(d, x_mate, x_send, x_recv, True).wait_recv()
        onward(d, False).start()

    arrived = [0]
    for d in RING:
        along_y(d, True).wait_recv()
        if d not in DIRECT:
            to_mate(d, x_mate, x_send, x_recv, False).start()
        to_mate(d, core_mate, c_send, c_recv, False).start()
        arrived.append(d)
        if len(arrived) > LAG:
            ready(arrived.pop(0))
    for d in arrived:
        ready(d)

    for load in loads[10:]:
        load.wait()
    for d in (0,) + RING:
        to_mate(d, core_mate, c_send, c_recv, True).wait_recv()
        onward(d, True).wait_recv()

    rank_of = lax.broadcasted_iota(jnp.int32, (RANK, MEMBERS), 0)

    def project(g, carry):
        for i in range(FAR_GROUP):
            b = g * FAR_GROUP + i
            made = jnp.dot(right[b], slips[far_cols[0, 0, b]], preferred_element_type=F32)
            coeffs[b] = jnp.where(rank_of < far_rank[0, 0, b], made, 0.0).astype(BF16)
        return carry

    def near_sum(g, carry):
        for i in range(GROUP):
            b = g * GROUP + i
            term = jnp.dot(near[b], slips[near_cols[0, 0, b]], preferred_element_type=F32)
            acc[1 + b] = term * near_scale[0, 0, b] + acc[chain[1 + b]]
        return carry

    def far_sum(g, carry):
        for i in range(FAR_GROUP):
            b = g * FAR_GROUP + i
            term = lax.dot_general(left[b], coeffs[b], (((0,), (0,)), ((), ())), preferred_element_type=F32)
            acc[1 + NEAR + b] = term * far_scale[0, 0, b] + acc[chain[1 + NEAR + b]]
        return carry

    lax.fori_loop(0, FAR // FAR_GROUP, project, 0)
    lax.fori_loop(0, NEAR // GROUP, near_sum, 0)
    lax.fori_loop(0, FAR // FAR_GROUP, far_sum, 0)

    def offset(j):
        return 4 + ((j + 1) // 2) * (1 - 2 * (j % 2))

    def part(j, half, r):
        owner = 2 * mod(z + offset(j), 8) + half
        return acc[last[r], pl.ds(pl.multiple_of(owner * BRICK, BRICK), BRICK), :]

    def pair(j):
        return copy(x_out.at[j], x_in.at[j], p_send.at[j], p_recv.at[j], s, far_mate)

    def along_z(j):
        return copy(z_out.at[j], z_in.at[j], z_send.at[j], z_recv.at[j], s, 2 * mod(z + offset(j), 8) + x_hi)

    def send_pair(j, carry):
        for r in range(BRICK):
            x_out[j, r] = part(j, 1 - x_hi, r).astype(BF16)
        pair(j).start()
        return carry

    def send_z(j, carry):
        pair(j).wait_recv()
        for r in range(BRICK):
            z_out[j, r] = (part(j, x_hi, r) + x_in[j, r].astype(F32)).astype(BF16)
        along_z(j).start()
        return carry

    def geometry(j, carry):
        for i in range(4):
            edges(4 * j + i)
        for i in range(3):
            wets[3 * j + i] = spread(compact[1, pl.ds(3 * j + i, 1), :], BRICK)
        return carry

    def add_z(j, carry):
        along_z(j).wait_recv()
        for r in range(BRICK):
            uplift[r] = uplift[r] + z_in[j, r].astype(F32)
        return carry

    lax.fori_loop(0, 8, send_pair, 0)
    for i in range(8):
        depth_copy(i).wait_recv()
    lane = lax.broadcasted_iota(jnp.int32, (BRICK, 128), 1)
    west_ok, east_ok = f > 0, f < FAULT - 1
    for dy, place in ((-1, 0), (0, TOP), (1, TOP + BRICK)):
        row_ok = (s + dy >= 0) & (s + dy < SEA)
        k = (dy + 1) * 3
        west = jnp.where((lane >= 8) & (lane < 16) & west_ok, depths[k], 0.0)
        east_side = jnp.where((lane < 8) & east_ok, depths[k + 2], 0.0)
        band = pltpu.roll(west, 120, 1) + pltpu.roll(depths[k + 1], 8, 1) + pltpu.roll(east_side, 24, 1)
        band = jnp.where(row_ok, band, 0.0)
        rows = band[BRICK - STEPS :] if dy < 0 else band[:STEPS] if dy > 0 else band
        compact[0, place : place + rows.shape[0], :] = rows
    compact[0, ROWS:, :] = jnp.zeros((32 - ROWS, 128), F32)
    compact[1] = jnp.zeros((32, 128), F32)
    compact[1, :BRICK, :BRICK] = wet_here
    eye = lax.broadcasted_iota(jnp.int32, (COLS, 128), 1) == lax.broadcasted_iota(jnp.int32, (COLS, 128), 0)

    def spread(row, width):
        kept = jnp.where(eye[:width], jnp.broadcast_to(row, (width, 128)), 0.0)
        return jnp.broadcast_to(jnp.sum(kept, axis=1, keepdims=True), (width, 128))

    def edges(i):
        here = compact[0, pl.ds(i, 1), :]
        east[i] = spread(GAIN * jnp.minimum(here, pltpu.roll(here, 127, 1)), COLS)
        north[i] = spread(GAIN * jnp.minimum(here, compact[0, pl.ds(i + 1, 1), :]), COLS)

    lax.fori_loop(0, 7, send_z, 0)
    lax.fori_loop(0, 7, geometry, 0)
    pair(7).wait_recv()
    for r in range(BRICK):
        uplift[r] = part(7, x_hi, r) + x_in[7, r].astype(F32)
    lax.fori_loop(0, 7, add_z, 0)
    out_uplift = pltpu.make_async_copy(uplift, both_hbm.at[0], out_sem.at[0])
    out_uplift.start()
    for r in range(BRICK):
        h[TOP + r, LEFT : LEFT + BRICK, :] = uplift[r] * wets[r]

    def span(i):
        dy, dx = NEIGHBOURS[i]
        tall, wide = (BRICK if dy == 0 else STEPS), (BRICK if dx == 0 else 8)
        src_y, dst_y = {-1: (TOP + BRICK - STEPS, 0), 0: (TOP, TOP), 1: (TOP, TOP + BRICK)}[dy]
        src_x, dst_x = {-1: (LEFT + BRICK - 8, 0), 0: (LEFT, LEFT), 1: (LEFT, LEFT + BRICK)}[dx]
        rows = 8 * tall
        src = (slice(src_y, src_y + tall), slice(src_x, src_x + wide), slice(None))
        dst = (slice(dst_y, dst_y + tall), slice(dst_x, dst_x + wide), slice(None))
        return dx, rows, src, dst

    def halo(i):
        dy, dx = NEIGHBOURS[i]
        _, rows, src, dst = span(i)
        to_sea, to_fault = mod(s - dy, SEA), mod(f - dx, FAULT)
        if dx == 0:
            return copy(h.at[src], h.at[dst], h_send.at[i], h_recv.at[i], to_sea, to_fault)
        return copy(strip_out.at[i, :rows], strip_in.at[i, :rows], h_send.at[i], h_recv.at[i], to_sea, to_fault)

    for i in range(8):
        dx, rows, src, _ = span(i)
        if dx:
            strip_out[i, :rows] = h[src].reshape(rows, MEMBERS).astype(BF16)
        halo(i).start()
    e[...] = jnp.zeros(e.shape, F32)
    n[...] = jnp.zeros(n.shape, F32)
    for d in RING:
        along_y(d, False).wait_send()
    for d in (0,) + RING:
        to_mate(d, x_mate, x_send, x_recv, False).wait_send()
        to_mate(d, core_mate, c_send, c_recv, False).wait_send()
        onward(d, False).wait_send()
    for i in range(8):
        depth_copy(i).wait_send()
    for j in range(8):
        pair(j).wait_send()
    for j in range(7):
        along_z(j).wait_send()
    for i in range(8):
        dx, rows, _, dst = span(i)
        halo(i).wait()
        if dx:
            h[dst] = strip_in[i, :rows].astype(F32).reshape(rows // 8, 8, MEMBERS)

    for step in range(STEPS):

        def row(i, below):
            here = h[i]
            flow_n = n[i] + (h[i + 1] - here)
            flow_e = e[i] + (pltpu.roll(here, COLS - 1, 0) - here)
            n[i] = flow_n
            e[i] = flow_e
            flux_n = north[i] * flow_n
            flux_e = east[i] * flow_e
            h[i] = here + (flux_e - pltpu.roll(flux_e, 1, 0) + flux_n - below)
            return flux_n

        def first(i):
            flow_n = n[i] + (h[i + 1] - h[i])
            n[i] = flow_n
            return north[i] * flow_n

        lax.fori_loop(step + 1, ROWS - 1 - step, row, first(step))
    out_level = pltpu.make_async_copy(h.at[TOP : TOP + BRICK, LEFT : LEFT + BRICK, :], both_hbm.at[1], out_sem.at[1])
    out_level.start()
    out_level.wait()
    out_uplift.wait()


def on_device(*args):
    hbm = pl.BlockSpec(memory_space=pltpu.HBM)
    field = pltpu.VMEM((ROWS, COLS, MEMBERS), F32)
    dma = pltpu.SemaphoreType.DMA
    brick = jax.ShapeDtypeStruct((BRICK, BRICK, MEMBERS), F32)
    made = pl.pallas_call(
        kernel,
        out_shape=jax.ShapeDtypeStruct((2, BRICK, BRICK, MEMBERS), F32),
        in_specs=[hbm] * 13,
        out_specs=hbm,
        scratch_shapes=[
            pltpu.VMEM((BRICK, BRICK, MEMBERS), F32),
            pltpu.VMEM((128, MEMBERS), BF16),
            *(pltpu.SMEM((1, 1, NEAR), kind) for kind in (jnp.int32, jnp.int32, F32)),
            *(pltpu.SMEM((1, 1, FAR), kind) for kind in (jnp.int32, jnp.int32, jnp.int32, F32)),
            pltpu.VMEM((BRICK, BRICK), F32),
            pltpu.VMEM((BRICK, BRICK), jnp.int32),
            pltpu.VMEM((LEAVES, LEAF, MEMBERS), BF16),
            pltpu.VMEM((NEAR, LEAF, LEAF), BF16),
            pltpu.VMEM((FAR, RANK, LEAF), BF16),
            pltpu.VMEM((FAR, RANK, LEAF), BF16),
            pltpu.VMEM((FAR, RANK, MEMBERS), BF16),
            pltpu.VMEM((1 + NEAR + FAR, LEAF, MEMBERS), F32),
            pltpu.SMEM((1 + NEAR + FAR,), jnp.int32),
            pltpu.SMEM((LEAVES,), jnp.int32),
            pltpu.VMEM((8, BRICK, BRICK, MEMBERS), BF16),
            pltpu.VMEM((8, BRICK, BRICK, MEMBERS), BF16),
            pltpu.VMEM((7, BRICK, BRICK, MEMBERS), BF16),
            pltpu.VMEM((7, BRICK, BRICK, MEMBERS), BF16),
            pltpu.VMEM((9, BRICK, 128), F32),
            pltpu.VMEM((2, 32, 128), F32),
            pltpu.VMEM((21, BRICK, MEMBERS), F32),
            pltpu.VMEM((8, 8 * BRICK, MEMBERS), BF16), pltpu.VMEM((8, 8 * BRICK, MEMBERS), BF16),
            field, field, field, field, field,
            dma((13,)),
            dma((8,)), dma((8,)), dma((8,)), dma((8,)), dma((8,)), dma((8,)), dma((8,)), dma((8,)),
            dma((8,)), dma((8,)),
            dma((8,)), dma((8,)), dma((7,)), dma((7,)), dma((8,)), dma((8,)), dma((2,)),
        ],
        compiler_params=pltpu.CompilerParams(
            collective_id=0, has_side_effects=True, vmem_limit_bytes=62 * 2**20
        ),
        name="forecast",
    )(*args)
    return made[0], made[1]


def solution(mesh):
    blocks = P("sea", "fault", None, None, None)
    lists = P("sea", "fault", None)
    cells = P("sea", "fault")
    return jax.shard_map(
        on_device,
        mesh=mesh,
        in_specs=(
            P(("fault", "sea"), None), blocks, lists, lists, lists, blocks, blocks, lists, lists, lists, lists, cells, cells,
        ),
        out_specs=(lists, lists),
        check_vma=False,
    )
```

time: 76.3 us -> 58.2 us (0.76)
  local copies, waits for them, and re-layouts: 11.4 us -> 1.69 us
  Pallas kernels: 63.4 us -> 55.7 us
    unnamed x28 -> x0, local copies, waits for them, and re-layouts: 11.4 us -> none
    pallas_call x1, Pallas kernels: 63.4 us -> 55.7 us  [on_device(): pl.pallas_call(kernel, out_shape=jax.ShapeDtypeStruct((2, BRICK, BRICK, M...]
    squeeze x0 -> x1, local copies, waits for them, and re-layouts: none -> 1.69 us  [on_device(): return (made[0], made[1])]
where the time goes in v2:
time: 58.2 us; the launch traced here: 58.1 us
  Pallas kernels  55.7 us (96%)
  local copies, waits for them, and re-layouts  1.69 us (3%)
  between operations  0.64 us (1%)
    pallas_call x1, Pallas kernels, on_device(): pl.pallas_call(kernel, out_shape=jax.ShapeDtypeStruct((2, BRICK, BRICK, M...  55.7 us
    squeeze x1, local copies, waits for them, and re-layouts, on_device(): return (made[0], made[1])  1.69 us

profile of v2, /device:TPU:1, one launch (start us, length us, event | category | flops | bytes accessed | tf_op | source)
XLA Modules:
  0.0 58.1 jit_solution(17075592189487228793)
XLA Ops:
  0.6 55.7 %forecast.1 = f32[2,16,16,128]{3,2,1,0:T(8,128)} custom-call(bf16[128,128]{1,0:T(8,128)(2,1)} %slip_hbm.1, bf16[1,1,8,256,256]{4,3,2,1,0:T(8,128)(2,1)} %near_hbm.1, s32[1,1,8]{2,1,0:T(1,128)} %near_rows_hbm.1, s32[1,1,8]{2,1,0:T(1,128)} %near_cols_hbm.1, f32[1,1,8]{2,1,0:T(1,128)} %near_scale_hbm.1, bf16[1,1,24,48,256]{4,3,2,1,0:T(8,128)(2,1)} %left_hbm.1, ...), custom_call_target="tpu_custom_call" | custom-call | tf_op jit(solution)/shard_map/forecast/pallas_call | solution.py:333
  56.4 1.7 %slice_bitcast_fusion = (f32[16,16,128]{2,1,0:T(8,128)}, f32[16,16,128]{2,1,0:T(8,128)}) fusion(f32[2,16,16,128]{3,2,1,0:T(8,128)} %forecast.1), kind=kLoop, calls=%fused_computation | loop fusion | bytes 524288 | tf_op jit(solution)/shard_map/squeeze | solution.py:372

commit v3 on v2

--- a/solution.py
+++ b/solution.py
@@ -20,7 +20,7 @@
 TOP, LEFT = STEPS, 8
 NEIGHBOURS = [(dy, dx) for dy in (-1, 0, 1) for dx in (-1, 0, 1) if (dy, dx) != (0, 0)]
 RING = (1, 7, 2, 6, 3, 5, 4)
-GROUP = 8
+TALL = 4
 FAR_GROUP = 24
 DIRECT = (4,)
 LAG = 4
@@ -33,11 +33,11 @@
 def kernel(
     slip_hbm, near_hbm, near_rows_hbm, near_cols_hbm, near_scale_hbm, left_hbm, right_hbm, far_rows_hbm, far_cols_hbm,
     far_rank_hbm, far_scale_hbm, depth_hbm, wet_hbm,
-    both_hbm,
-    uplift, slip, near_rows, near_cols, near_scale, far_rows, far_cols, far_rank, far_scale, depth, wet,
-    slips, near, left, right, coeffs, acc, chain, last, x_out, x_in, z_out, z_in, depths, compact, wets, strip_out, strip_in, east, north, h, e, n,
+    both,
+    slip, near_rows, near_cols, near_scale, far_rows, far_cols, far_rank, far_scale, depth, wet,
+    slips, turned, near, left, right, coeffs, acc, chain, last, x_out, x_in, z_out, z_in, depths, compact, wets, strip_out, strip_in, east, north, h, e, n,
     load_sem, y_send, y_recv, x_send, x_recv, c_send, c_recv, k_send, k_recv, d_send, d_recv,
-    p_send, p_recv, z_send, z_recv, h_send, h_recv, out_sem,
+    p_send, p_recv, z_send, z_recv, h_send, h_recv,
 ):
     s, f = lax.axis_index("sea"), lax.axis_index("fault")
     y, x_lo, core = s // 4, (s // 2) % 2, s % 2
@@ -62,7 +62,7 @@
         (slip_hbm, slip), (depth_hbm, depth), (wet_hbm, wet), (near_rows_hbm, near_rows), (far_rows_hbm, far_rows),
         (near_cols_hbm, near_cols), (far_cols_hbm, far_cols), (far_rank_hbm, far_rank),
         (near_scale_hbm, near_scale), (far_scale_hbm, far_scale),
-        (right_hbm.at[0, 0], right), (near_hbm.at[0, 0], near), (left_hbm.at[0, 0], left),
+        (right_hbm.at[0, 0], right), (near_hbm.at[:, :, 0], near.at[0]), (near_hbm.at[:, :, 1], near.at[1]), (left_hbm.at[0, 0], left),
     )
     loads = [pltpu.make_async_copy(src, dst, load_sem.at[i]) for i, (src, dst) in enumerate(pairs)]
     for load in loads:
@@ -111,7 +111,7 @@
     for i in range(8):
         depth_copy(i).start()
 
-    acc[0] = jnp.zeros((LEAF, MEMBERS), F32)
+    acc[0] = jnp.zeros((2, LEAF // 2, MEMBERS), F32)
     for r in range(LEAVES):
         last[r] = 0
 
@@ -130,6 +130,16 @@
     lax.fori_loop(0, NEAR, link(near_rows, 1), 0)
     lax.fori_loop(0, FAR, link(far_rows, 1 + NEAR), 0)
 
+    def turn(g, carry):
+        for i in range(8):
+            b = 8 * g + i
+            cells = left[b].T.reshape(8, 2, BRICK, RANK)
+            for half in range(2):
+                turned[b, half] = cells[:, half].reshape(LEAF // 2, RANK)
+        return carry
+
+    loads[13].wait()
+    lax.fori_loop(0, FAR // 8, turn, 0)
     def ready(d):
         to_mate(d, x_mate, x_send, x_recv, True).wait_recv()
         onward(d, False).start()
@@ -146,7 +156,7 @@
     for d in arrived:
         ready(d)
 
-    for load in loads[10:]:
+    for load in loads[10:13]:
         load.wait()
     for d in (0,) + RING:
         to_mate(d, core_mate, c_send, c_recv, True).wait_recv()
@@ -161,30 +171,24 @@
             coeffs[b] = jnp.where(rank_of < far_rank[0, 0, b], made, 0.0).astype(BF16)
         return carry
 
-    def near_sum(g, carry):
-        for i in range(GROUP):
-            b = g * GROUP + i
-            term = jnp.dot(near[b], slips[near_cols[0, 0, b]], preferred_element_type=F32)
-            acc[1 + b] = term * near_scale[0, 0, b] + acc[chain[1 + b]]
-        return carry
-
-    def far_sum(g, carry):
-        for i in range(FAR_GROUP):
-            b = g * FAR_GROUP + i
-            term = lax.dot_general(left[b], coeffs[b], (((0,), (0,)), ((), ())), preferred_element_type=F32)
-            acc[1 + NEAR + b] = term * far_scale[0, 0, b] + acc[chain[1 + NEAR + b]]
-        return carry
+    def sums(half):
+        for b in range(NEAR):
+            block = near[half, b].reshape(LEAF // 2, LEAF)
+            term = jnp.dot(block, slips[near_cols[0, 0, b]], preferred_element_type=F32)
+            acc[1 + b, half] = term * near_scale[0, 0, b] + acc[chain[1 + b], half]
+        for b in range(FAR):
+            term = jnp.dot(turned[b, half], coeffs[b], preferred_element_type=F32)
+            acc[1 + NEAR + b, half] = term * far_scale[0, 0, b] + acc[chain[1 + NEAR + b], half]
 
     lax.fori_loop(0, FAR // FAR_GROUP, project, 0)
-    lax.fori_loop(0, NEAR // GROUP, near_sum, 0)
-    lax.fori_loop(0, FAR // FAR_GROUP, far_sum, 0)
+    sums(1 - x_hi)
 
     def offset(j):
         return 4 + ((j + 1) // 2) * (1 - 2 * (j % 2))
 
     def part(j, half, r):
-        owner = 2 * mod(z + offset(j), 8) + half
-        return acc[last[r], pl.ds(pl.multiple_of(owner * BRICK, BRICK), BRICK), :]
+        place = pl.multiple_of(mod(z + offset(j), 8) * BRICK, BRICK)
+        return acc[last[r], half, pl.ds(place, BRICK), :]
 
     def pair(j):
         return copy(x_out.at[j], x_in.at[j], p_send.at[j], p_recv.at[j], s, far_mate)
@@ -215,10 +219,11 @@
     def add_z(j, carry):
         along_z(j).wait_recv()
         for r in range(BRICK):
-            uplift[r] = uplift[r] + z_in[j, r].astype(F32)
+            both[0, r] = both[0, r] + z_in[j, r].astype(F32)
         return carry
 
     lax.fori_loop(0, 8, send_pair, 0)
+    sums(x_hi)
     for i in range(8):
         depth_copy(i).wait_recv()
     lane = lax.broadcasted_iota(jnp.int32, (BRICK, 128), 1)
@@ -250,12 +255,10 @@
     lax.fori_loop(0, 7, geometry, 0)
     pair(7).wait_recv()
     for r in range(BRICK):
-        uplift[r] = part(7, x_hi, r) + x_in[7, r].astype(F32)
+        both[0, r] = part(7, x_hi, r) + x_in[7, r].astype(F32)
     lax.fori_loop(0, 7, add_z, 0)
-    out_uplift = pltpu.make_async_copy(uplift, both_hbm.at[0], out_sem.at[0])
-    out_uplift.start()
     for r in range(BRICK):
-        h[TOP + r, LEFT : LEFT + BRICK, :] = uplift[r] * wets[r]
+        h[TOP + r, LEFT : LEFT + BRICK, :] = both[0, r] * wets[r]
 
     def span(i):
         dy, dx = NEIGHBOURS[i]
@@ -301,28 +304,27 @@
             h[dst] = strip_in[i, :rows].astype(F32).reshape(rows // 8, 8, MEMBERS)
 
     for step in range(STEPS):
-
-        def row(i, below):
-            here = h[i]
-            flow_n = n[i] + (h[i + 1] - here)
-            flow_e = e[i] + (pltpu.roll(here, COLS - 1, 0) - here)
-            n[i] = flow_n
-            e[i] = flow_e
-            flux_n = north[i] * flow_n
-            flux_e = east[i] * flow_e
-            h[i] = here + (flux_e - pltpu.roll(flux_e, 1, 0) + flux_n - below)
-            return flux_n
-
-        def first(i):
-            flow_n = n[i] + (h[i + 1] - h[i])
-            n[i] = flow_n
-            return north[i] * flow_n
-
-        lax.fori_loop(step + 1, ROWS - 1 - step, row, first(step))
-    out_level = pltpu.make_async_copy(h.at[TOP : TOP + BRICK, LEFT : LEFT + BRICK, :], both_hbm.at[1], out_sem.at[1])
-    out_level.start()
-    out_level.wait()
-    out_uplift.wait()
+        def rows(i, count, below):
+            here = [h[i + k] for k in range(count + 1)]
+            flows = [n[i + k] + (here[k + 1] - here[k]) for k in range(count)]
+            eastward = [e[i + k] + (pltpu.roll(here[k], COLS - 1, 0) - here[k]) for k in range(count)]
+            fluxes = [below] + [north[i + k] * flows[k] for k in range(count)]
+            sideways = [east[i + k] * eastward[k] for k in range(count)]
+            change = [side - pltpu.roll(side, 1, 0) for side in sideways]
+            for k in range(count):
+                n[i + k] = flows[k]
+                e[i + k] = eastward[k]
+                h[i + k] = here[k] + (change[k] + (fluxes[k + 1] - fluxes[k]))
+            return fluxes[-1]
+
+        count = ROWS - 2 - 2 * step
+        flow = n[step] + (h[step + 1] - h[step])
+        n[step] = flow
+        below = north[step] * flow
+        below = lax.fori_loop(0, count // TALL, lambda g, carry: rows(step + 1 + TALL * g, TALL, carry), below)
+        if count % TALL:
+            rows(ROWS - 1 - step - count % TALL, count % TALL, below)
+    both[1] = h[TOP : TOP + BRICK, LEFT : LEFT + BRICK, :]
 
 
 def on_device(*args):
@@ -330,24 +332,25 @@
     field = pltpu.VMEM((ROWS, COLS, MEMBERS), F32)
     dma = pltpu.SemaphoreType.DMA
     brick = jax.ShapeDtypeStruct((BRICK, BRICK, MEMBERS), F32)
+    near = args[1].reshape(NEAR, 8, 2, BRICK, LEAF)
     made = pl.pallas_call(
         kernel,
-        out_shape=jax.ShapeDtypeStruct((2, BRICK, BRICK, MEMBERS), F32),
+        out_shape=pltpu.VMEM((2, BRICK, BRICK, MEMBERS), F32),
         in_specs=[hbm] * 13,
-        out_specs=hbm,
+        out_specs=pl.BlockSpec(memory_space=pltpu.VMEM),
         scratch_shapes=[
-            pltpu.VMEM((BRICK, BRICK, MEMBERS), F32),
             pltpu.VMEM((128, MEMBERS), BF16),
             *(pltpu.SMEM((1, 1, NEAR), kind) for kind in (jnp.int32, jnp.int32, F32)),
             *(pltpu.SMEM((1, 1, FAR), kind) for kind in (jnp.int32, jnp.int32, jnp.int32, F32)),
             pltpu.VMEM((BRICK, BRICK), F32),
             pltpu.VMEM((BRICK, BRICK), jnp.int32),
             pltpu.VMEM((LEAVES, LEAF, MEMBERS), BF16),
-            pltpu.VMEM((NEAR, LEAF, LEAF), BF16),
+            pltpu.VMEM((FAR, 2, LEAF // 2, RANK), BF16),
+            pltpu.VMEM((2, NEAR, 8, BRICK, LEAF), BF16),
             pltpu.VMEM((FAR, RANK, LEAF), BF16),
             pltpu.VMEM((FAR, RANK, LEAF), BF16),
             pltpu.VMEM((FAR, RANK, MEMBERS), BF16),
-            pltpu.VMEM((1 + NEAR + FAR, LEAF, MEMBERS), F32),
+            pltpu.VMEM((1 + NEAR + FAR, 2, LEAF // 2, MEMBERS), F32),
             pltpu.SMEM((1 + NEAR + FAR,), jnp.int32),
             pltpu.SMEM((LEAVES,), jnp.int32),
             pltpu.VMEM((8, BRICK, BRICK, MEMBERS), BF16),
@@ -359,16 +362,16 @@
             pltpu.VMEM((21, BRICK, MEMBERS), F32),
             pltpu.VMEM((8, 8 * BRICK, MEMBERS), BF16), pltpu.VMEM((8, 8 * BRICK, MEMBERS), BF16),
             field, field, field, field, field,
-            dma((13,)),
+            dma((14,)),
             dma((8,)), dma((8,)), dma((8,)), dma((8,)), dma((8,)), dma((8,)), dma((8,)), dma((8,)),
             dma((8,)), dma((8,)),
-            dma((8,)), dma((8,)), dma((7,)), dma((7,)), dma((8,)), dma((8,)), dma((2,)),
+            dma((8,)), dma((8,)), dma((7,)), dma((7,)), dma((8,)), dma((8,)),
         ],
         compiler_params=pltpu.CompilerParams(
             collective_id=0, has_side_effects=True, vmem_limit_bytes=62 * 2**20
         ),
         name="forecast",
-    )(*args)
+    )(args[0], near, *args[2:])
     return made[0], made[1]
 
 

time: 58.2 us -> 55.5 us (0.954)
  Pallas kernels: 55.7 us -> 54 us
  local copies, waits for them, and re-layouts: 1.69 us -> 0.72 us
    pallas_call x1, Pallas kernels: 55.7 us -> 54 us  [on_device(): pl.pallas_call(kernel, out_shape=pltpu.VMEM((2, BRICK, BRICK, MEMBERS), F...]
    squeeze x1, local copies, waits for them, and re-layouts: 1.69 us -> 0.72 us  [on_device(): return (made[0], made[1])]
where the time goes in v3:
time: 55.5 us; the launch traced here: 55.4 us
  Pallas kernels  54 us (97%)
  local copies, waits for them, and re-layouts  0.72 us (1%)
  between operations  0.64 us (1%)
    pallas_call x1, Pallas kernels, on_device(): pl.pallas_call(kernel, out_shape=pltpu.VMEM((2, BRICK, BRICK, MEMBERS), F...  54 us

profile of v3, /device:TPU:1, one launch (start us, length us, event | category | flops | bytes accessed | tf_op | source)
XLA Modules:
  0.0 55.4 jit_solution(2064413271188825515)
XLA Ops:
  0.6 54.0 %forecast.1 = f32[2,16,16,128]{3,2,1,0:T(8,128)S(1)} custom-call(bf16[128,128]{1,0:T(8,128)(2,1)} %slip_hbm.1, bf16[8,8,2,16,256]{4,3,2,1,0:T(8,128)(2,1)} %bitcast.5, s32[1,1,8]{2,1,0:T(1,128)} %near_rows_hbm.1, s32[1,1,8]{2,1,0:T(1,128)} %near_cols_hbm.1, f32[1,1,8]{2,1,0:T(1,128)} %near_scale_hbm.1, bf16[1,1,24,48,256]{4,3,2,1,0:T(8,128)(2,1)} %left_hbm.1, ...), custom_call_target="tpu_custom_call" | custom-call | tf_op jit(solution)/shard_map/forecast/pallas_call | solution.py:336
  54.6 0.7 %slice_bitcast_fusion = (f32[16,16,128]{2,1,0:T(8,128)}, f32[16,16,128]{2,1,0:T(8,128)}) fusion(f32[2,16,16,128]{3,2,1,0:T(8,128)S(1)} %forecast.1), kind=kLoop, calls=%fused_computation | loop fusion | bytes 524288 | tf_op jit(solution)/shard_map/squeeze | solution.py:375

commit v4 on v3

--- a/solution.py
+++ b/solution.py
@@ -18,7 +18,7 @@
 BRICK = 16
 ROWS, COLS = BRICK + 2 * STEPS, BRICK + 16
 TOP, LEFT = STEPS, 8
-NEIGHBOURS = [(dy, dx) for dy in (-1, 0, 1) for dx in (-1, 0, 1) if (dy, dx) != (0, 0)]
+NEIGHBOURS = [(-1, 0), (1, 0), (-1, -1), (-1, 1), (1, -1), (1, 1), (0, -1), (0, 1)]
 RING = (1, 7, 2, 6, 3, 5, 4)
 TALL = 4
 FAR_GROUP = 24

time: 55.5 us -> 55.4 us (level)
  no operation moved by 1% of the time
where the time goes in v4:
time: 55.4 us; the launch traced here: 55.2 us
  Pallas kernels  53.9 us (97%)
  local copies, waits for them, and re-layouts  0.72 us (1%)
  between operations  0.64 us (1%)
    pallas_call x1, Pallas kernels, on_device(): pl.pallas_call(kernel, out_shape=pltpu.VMEM((2, BRICK, BRICK, MEMBERS), F...  53.9 us

profile of v4, /device:TPU:1, one launch (start us, length us, event | category | flops | bytes accessed | tf_op | source)
XLA Modules:
  0.0 55.2 jit_solution(17064510348393784266)
XLA Ops:
  0.6 53.9 %forecast.1 = f32[2,16,16,128]{3,2,1,0:T(8,128)S(1)} custom-call(bf16[128,128]{1,0:T(8,128)(2,1)} %slip_hbm.1, bf16[8,8,2,16,256]{4,3,2,1,0:T(8,128)(2,1)} %bitcast.5, s32[1,1,8]{2,1,0:T(1,128)} %near_rows_hbm.1, s32[1,1,8]{2,1,0:T(1,128)} %near_cols_hbm.1, f32[1,1,8]{2,1,0:T(1,128)} %near_scale_hbm.1, bf16[1,1,24,48,256]{4,3,2,1,0:T(8,128)(2,1)} %left_hbm.1, ...), custom_call_target="tpu_custom_call" | custom-call | tf_op jit(solution)/shard_map/forecast/pallas_call | solution.py:336
  54.5 0.7 %slice_bitcast_fusion = (f32[16,16,128]{2,1,0:T(8,128)}, f32[16,16,128]{2,1,0:T(8,128)}) fusion(f32[2,16,16,128]{3,2,1,0:T(8,128)S(1)} %forecast.1), kind=kLoop, calls=%fused_computation | loop fusion | bytes 524288 | tf_op jit(solution)/shard_map/squeeze | solution.py:375

commit v5 on v4

--- a/solution.py
+++ b/solution.py
@@ -184,7 +184,13 @@
     sums(1 - x_hi)
 
     def offset(j):
-        return 4 + ((j + 1) // 2) * (1 - 2 * (j % 2))
+        k = (j + 1) // 2
+        return 4 + (k + ((k // 2) % 2) * (5 - 2 * k)) * (1 - 2 * (j % 2))
+
+    def relay(half):
+        rows = slice(8 * half, 8 * half + 8)
+        to_fault = 2 * mod(z + (2 if half else 6), 8) + x_hi
+        return copy(z_out.at[0, rows], z_in.at[0, rows], z_send.at[7 * half], z_recv.at[7 * half], s, to_fault)
 
     def part(j, half, r):
         place = pl.multiple_of(mod(z + offset(j), 8) * BRICK, BRICK)
@@ -202,10 +208,16 @@
         pair(j).start()
         return carry
 
-    def send_z(j, carry):
+    def pair_sum(j, extra):
         pair(j).wait_recv()
         for r in range(BRICK):
-            z_out[j, r] = (part(j, x_hi, r) + x_in[j, r].astype(F32)).astype(BF16)
+            both_sides = part(j, x_hi, r) + x_in[j, r].astype(F32)
+            if r in extra:
+                both_sides = both_sides + z_in[0, r].astype(F32)
+            z_out[j, r] = both_sides.astype(BF16)
+
+    def send_z(j, carry):
+        pair_sum(j, ())
         along_z(j).start()
         return carry
 
@@ -251,12 +263,19 @@
         east[i] = spread(GAIN * jnp.minimum(here, pltpu.roll(here, 127, 1)), COLS)
         north[i] = spread(GAIN * jnp.minimum(here, compact[0, pl.ds(i + 1, 1), :]), COLS)
 
-    lax.fori_loop(0, 7, send_z, 0)
+    pair_sum(0, ())
+    for half in range(2):
+        relay(half).start()
+    lax.fori_loop(1, 5, send_z, 0)
+    for j, half in ((5, 1), (6, 0)):
+        relay(half).wait_recv()
+        pair_sum(j, range(8 * half, 8 * half + 8))
+        along_z(j).start()
     lax.fori_loop(0, 7, geometry, 0)
     pair(7).wait_recv()
     for r in range(BRICK):
         both[0, r] = part(7, x_hi, r) + x_in[7, r].astype(F32)
-    lax.fori_loop(0, 7, add_z, 0)
+    lax.fori_loop(1, 7, add_z, 0)
     for r in range(BRICK):
         h[TOP + r, LEFT : LEFT + BRICK, :] = both[0, r] * wets[r]
 
@@ -295,7 +314,9 @@
         depth_copy(i).wait_send()
     for j in range(8):
         pair(j).wait_send()
-    for j in range(7):
+    for half in range(2):
+        relay(half).wait_send()
+    for j in range(1, 7):
         along_z(j).wait_send()
     for i in range(8):
         dx, rows, _, dst = span(i)
@@ -365,7 +386,7 @@
             dma((14,)),
             dma((8,)), dma((8,)), dma((8,)), dma((8,)), dma((8,)), dma((8,)), dma((8,)), dma((8,)),
             dma((8,)), dma((8,)),
-            dma((8,)), dma((8,)), dma((7,)), dma((7,)), dma((8,)), dma((8,)),
+            dma((8,)), dma((8,)), dma((8,)), dma((8,)), dma((8,)), dma((8,)),
         ],
         compiler_params=pltpu.CompilerParams(
             collective_id=0, has_side_effects=True, vmem_limit_bytes=62 * 2**20

time: 55.4 us -> 55 us (level)
  no operation moved by 1% of the time
where the time goes in v5:
time: 55 us; the launch traced here: 54.9 us
  Pallas kernels  53.6 us (97%)
  local copies, waits for them, and re-layouts  0.72 us (1%)
  between operations  0.64 us (1%)
    pallas_call x1, Pallas kernels, on_device(): pl.pallas_call(kernel, out_shape=pltpu.VMEM((2, BRICK, BRICK, MEMBERS), F...  53.6 us

profile of v5, /device:TPU:1, one launch (start us, length us, event | category | flops | bytes accessed | tf_op | source)
XLA Modules:
  0.0 54.9 jit_solution(9555426679131174647)
XLA Ops:
  0.6 53.6 %forecast.1 = f32[2,16,16,128]{3,2,1,0:T(8,128)S(1)} custom-call(bf16[128,128]{1,0:T(8,128)(2,1)} %slip_hbm.1, bf16[8,8,2,16,256]{4,3,2,1,0:T(8,128)(2,1)} %bitcast.5, s32[1,1,8]{2,1,0:T(1,128)} %near_rows_hbm.1, s32[1,1,8]{2,1,0:T(1,128)} %near_cols_hbm.1, f32[1,1,8]{2,1,0:T(1,128)} %near_scale_hbm.1, bf16[1,1,24,48,256]{4,3,2,1,0:T(8,128)(2,1)} %left_hbm.1, ...), custom_call_target="tpu_custom_call" | custom-call | tf_op jit(solution)/shard_map/forecast/pallas_call | solution.py:357
  54.2 0.7 %slice_bitcast_fusion = (f32[16,16,128]{2,1,0:T(8,128)}, f32[16,16,128]{2,1,0:T(8,128)}) fusion(f32[2,16,16,128]{3,2,1,0:T(8,128)S(1)} %forecast.1), kind=kLoop, calls=%fused_computation | loop fusion | bytes 524288 | tf_op jit(solution)/shard_map/squeeze | solution.py:396
